TPU v7x, 32 devices: a whole 2x2x4 slice. The times are simulated.
32 devices in a mesh: snap: 2 (over y), row: 4 (over z), col: 4 (over x, core).
Axes of the slice: x: 2, y: 2, z: 4, core: 2. Of those that a mesh axis runs over, the one named last changes fastest.
Arguments:
- orbitals: float32 [12288, 768], P(('snap', 'row', 'col')), parts along dimension 0, may hold values from -6 to 6
- screened: float32 [6, 6144, 6144], P('snap', 'row', 'col'), parts along dimension 0, may hold values from -0.0029296875 to 0.0029296875
- green_weight: float32 [6, 768], P('snap'), parts along dimension 0, may hold values from 0.05 to 1
- time_weight: float32 [3], replicated, may hold values from 0.3 to 1
Outputs:
- updated: float32 [12288, 768], P(('snap', 'row', 'col')), parts along dimension 0
There are 2 independent parts, one for each index of `snap`. A program takes and returns all parts, laid end to end along the dimension named above; an argument that names none is the same for every part. Nothing has to cross between parts.
All inputs are finite; a program needn't handle non-finite values.
Results may differ from a plain program's by a relative error of at most 0.00013.
Values sent between devices are 32-bit elements; how exact they have to be, the bound alone decides.
No kernel may reach another device: no remote copies, remote signals or barrier semaphores. Data moves between devices by JAX's collectives and lax.ppermute only.
A program may use at most 128 MiB of HBM per device.

v0:
```python
import functools

import jax
import jax.numpy as jnp
from jax import lax
from jax.experimental import pallas as pl
from jax.experimental.pallas import tpu as pltpu
from jax.sharding import PartitionSpec as P

PASSES = 2
LANES = 128
VMEM_BYTES = 32 * 2**20


def dot_t(a, b):
    return lax.dot_general(a, b, (((1,), (1,)), ((), ())), preferred_element_type=jnp.float32)


def dot_n(a, b):
    return lax.dot_general(a, b, (((1,), (0,)), ((), ())), preferred_element_type=jnp.float32)


def split(x):
    high = x.astype(jnp.bfloat16)
    return high, (x - high.astype(jnp.float32)).astype(jnp.bfloat16)


def apply_kernel(pieces, first, tiles, place, *refs):
    weight_ref, refs = refs[0], refs[1:]
    rows_refs, refs = refs[: len(tiles)], refs[len(tiles) :]
    cols_refs, refs = refs[:pieces], refs[pieces:]
    screened_refs, refs = refs[:pieces], refs[pieces:]
    out_ref, high_ref, low_ref = refs[-3:]
    times = weight_ref.shape[0]
    width = cols_refs[0].shape[0]
    i = pl.program_id(0)

    @pl.when(i == 0)
    def _():
        for p in range(pieces):
            here = pl.ds(p * width, width)
            high_ref[here, :], low_ref[here, :] = split(cols_refs[p][...])

    rows = rows_refs[0][...]
    start = 0
    for ref, count in zip(rows_refs[1:], tiles):
        start += count
        rows = jnp.where(i >= start, ref[...], rows)
    weighted = [split(rows * weight_ref[t, :][None, :]) for t in range(times)]
    high = jnp.concatenate([h for h, _ in weighted], axis=0)
    low = jnp.concatenate([l for _, l in weighted], axis=0)
    green = dot_t(high, high_ref[...]) + (dot_t(high, low_ref[...]) + dot_t(low, high_ref[...]))
    tile = rows.shape[0]
    mixed = None
    for t in range(times):
        term = green[t * tile : (t + 1) * tile] * jnp.concatenate([ref[t] for ref in screened_refs], axis=1)
        mixed = term if mixed is None else mixed + term
    high, low = split(mixed)
    applied = dot_n(high, high_ref[...]) + (dot_n(high, low_ref[...]) + dot_n(low, high_ref[...]))
    out_ref[...] = applied if first else refs[0][...] + applied


def apply_chunk(row_place, col_place, rows, pieces, weight, screened, partial_value, tile, after=()):
    orbitals = rows[0].shape[1]
    n = len(pieces)
    width = pieces[0].shape[0]
    times = weight.shape[0]
    tiles = [r.shape[0] // tile for r in rows]
    total = sum(tiles)
    n_rows = total * tile
    first = partial_value is None
    place = jnp.stack(list(row_place) + list(col_place)).astype(jnp.int32)
    tile_spec = pl.BlockSpec((tile, orbitals), lambda i, place: (i, 0))
    in_specs = [pl.BlockSpec((times, orbitals), lambda i, place: (0, 0))]
    start = 0
    for count in tiles:
        in_specs.append(
            pl.BlockSpec(
                (tile, orbitals),
                lambda i, place, s=start, c=count: (jnp.clip(i - s, 0, c - 1), 0),
            )
        )
        start += count
    in_specs += [pl.BlockSpec((width, orbitals), lambda i, place: (0, 0))] * n
    in_specs += [
        pl.BlockSpec((times, tile, width), lambda i, place, p=p: (0, place[i], place[total + p]))
        for p in range(n)
    ]
    args = [weight, *rows, *pieces] + [screened] * n
    if not first:
        in_specs.append(tile_spec)
        args.append(partial_value)
    aliases = {} if first else {len(args): 0}
    in_specs += [pl.BlockSpec(memory_space=pl.ANY)] * len(after)
    args += after
    return pl.pallas_call(
        functools.partial(apply_kernel, n, first, tiles),
        grid_spec=pltpu.PrefetchScalarGridSpec(
            num_scalar_prefetch=1,
            grid=(total,),
            in_specs=in_specs,
            out_specs=tile_spec,
            scratch_shapes=[pltpu.VMEM((n * width, orbitals), jnp.bfloat16)] * 2,
        ),
        out_shape=jax.ShapeDtypeStruct((n_rows, orbitals), jnp.float32),
        input_output_aliases=aliases,
        compiler_params=pltpu.CompilerParams(vmem_limit_bytes=VMEM_BYTES),
        cost_estimate=pl.CostEstimate(
            flops=2 * n_rows * n * width * orbitals * 3 * (times + 1),
            bytes_accessed=4 * (3 * n_rows * orbitals + times * n_rows * n * width),
            transcendentals=0,
        ),
        name="apply_chunk",
    )(place, *args)


def pick_kernel(n_in, sets, n_on, which, *refs):
    n_out = which.shape[0]
    outs, sem = refs[len(refs) - 1 - n_out * sets : -1], refs[-1]
    for s in range(sets):
        ins = refs[s * n_in : (s + 1) * n_in]
        for p in range(n_out):
            out, signal = outs[s * n_out + p], sem.at[s * n_out + p]
            if n_in == 1:
                pltpu.make_async_copy(ins[0].at[which[p]], out, signal).start()
                continue
            for j in range(n_in):

                @pl.when(which[p] == j)
                def _():
                    pltpu.make_async_copy(ins[j], out, signal).start()

    for p, out in enumerate(outs):
        source = refs[0].at[0] if n_in == 1 else refs[0]
        pltpu.make_async_copy(source, out, sem.at[p]).wait()


def pick(sets, which, handed=(), after=()):
    n_in, n_out, n_on = len(sets[0]), len(which), len(handed)
    values = [value for values in sets for value in values]
    total = n_out * len(sets)
    anywhere = pl.BlockSpec(memory_space=pl.ANY)
    shape = jax.ShapeDtypeStruct(values[0].shape[-2:], values[0].dtype)
    out = pl.pallas_call(
        functools.partial(pick_kernel, n_in, len(sets), n_on),
        grid_spec=pltpu.PrefetchScalarGridSpec(
            num_scalar_prefetch=1,
            grid=(),
            in_specs=[anywhere] * (len(values) + n_on + len(after)),
            out_specs=[anywhere] * n_on + [pl.BlockSpec(memory_space=pltpu.VMEM)] * total,
            scratch_shapes=[pltpu.SemaphoreType.DMA((total,))],
        ),
        out_shape=[shape] * (n_on + total),
        input_output_aliases={1 + len(values) + j: j for j in range(n_on)},
        cost_estimate=pl.CostEstimate(flops=0, bytes_accessed=8 * total * shape.size, transcendentals=0),
        name="pick",
    )(jnp.stack(which).astype(jnp.int32), *values, *handed, *after)
    picked = out[n_on:]
    return [picked[s * n_out : (s + 1) * n_out] for s in range(len(sets))], out[:n_on]


def swap(value, bit, n_col):
    return lax.ppermute(value, "col", [(i, i ^ bit) for i in range(n_col)])


def gather_relative(own, n_col):
    shards = {0: own}
    bit = n_col // 2
    while bit:
        for p, shard in list(shards.items()):
            shards[p ^ bit] = swap(shard, bit, n_col)
        bit //= 2
    return [shards[p] for p in range(n_col)]


def scatter_relative(parts, n_col):
    bit = 1
    held = dict(enumerate(parts))
    while bit < len(parts):
        held = {p: held[p] + swap(held[p ^ bit], bit, n_col) for p in held if not p & bit}
        bit *= 2
    return held[0]


def line_hops(found, hops, n_row):
    for hop in hops:
        for way in (1, -1):
            pairs = [(i, i + way) for i in range(n_row) if 0 <= i + way < n_row]
            found[way * hop] = lax.ppermute(found[way * (hop - 1)], "row", pairs)
    return found


def one_pass(chunks, screened, weight, n_row, n_col):
    row_index = lax.axis_index("row")
    col_index = lax.axis_index("col")
    n = len(chunks)
    half = n_col // 2
    shard = sum(chunk.shape[0] for chunk in chunks)
    tile = 8 * max(d for d in range(1, 49) if shard % (8 * d) == 0)
    there = [col_index ^ p for p in range(n_col)]
    away = [row_index - c + n_row - 1 for c in there]
    distances = range(1 - n_row, n_row)

    found = [line_hops({0: chunk}, range(1, n_row), n_row) for chunk in chunks[:2]]
    shards = gather_relative(jnp.concatenate(chunks, axis=0), n_col)
    picked, handed = pick([[f[d] for d in distances] for f in found], away, chunks[2:])

    place = [c * (shard // tile) + i for c in there for i in range(shard // tile)]
    cut = len(place) // 2
    pieces = []

    def apply(upper, k, partial_value, after=()):
        col_place = [c * n + k for c in there]
        rows = shards[half:] if upper else shards[:half]
        row_place = place[cut:] if upper else place[:cut]
        return apply_chunk(row_place, col_place, rows, pieces[k], weight, screened, partial_value, tile, after)

    low = high = None
    for k in range(n):
        if k >= 2:
            line = lax.all_gather(handed[k - 2], "row")
            (fetched,), _ = pick([[line]], there, (), (low,) if k == 2 else (high,))
            picked.append(fetched)
        pieces.append([picked[k][0]] + [swap(picked[k][p], p, n_col) for p in range(1, n_col)])
        high = apply(True, k, high)
        if k < max(n - 2, 1):
            low = apply(False, k, low)
    far = scatter_relative([high[p * shard : (p + 1) * shard] for p in range(half)], n_col)
    for k in range(max(n - 2, 1), n):
        low = apply(False, k, low, (far,))
    across = swap(far, half, n_col)
    new = []
    start = 0
    for chunk in chunks:
        here = [slice(p * shard + start, p * shard + start + chunk.shape[0]) for p in range(half)]
        near = scatter_relative([low[at] for at in here], n_col)
        new.append(chunk - (near + across[here[0]]))
        start += chunk.shape[0]
    return new


def one_pass_plain(own, screened, weight, n_row, n_col):
    factor = n_col // n_row
    width = screened.shape[2]
    row_index = lax.axis_index("row")
    col_index = lax.axis_index("col")
    rows = lax.all_gather(own, "col", axis=0, tiled=True)
    piece = lax.dynamic_slice_in_dim(rows, col_index % factor * width, width, 0)
    piece = jnp.where(row_index == col_index // factor, piece, jnp.zeros_like(piece))
    piece = lax.psum(piece, "row")
    tile = 8 * max(d for d in range(1, 33) if rows.shape[0] % (8 * d) == 0)
    row_place = list(jnp.arange(rows.shape[0] // tile, dtype=jnp.int32))
    partial_value = apply_chunk(
        row_place, [jnp.int32(0)], [rows], [piece], weight, screened, None, tile
    )
    return own - lax.psum_scatter(partial_value, "col", scatter_dimension=0, tiled=True)


def body(orbitals, screened, green_weight, time_weight):
    n_row = lax.axis_size("row")
    n_col = lax.axis_size("col")
    weight = green_weight * time_weight[:, None]
    shard = orbitals.shape[0]
    if n_row == n_col and n_col & (n_col - 1) == 0 and shard % LANES == 0:
        chunks = [orbitals[k : k + LANES] for k in range(0, shard, LANES)]
        for _ in range(PASSES):
            chunks = one_pass(chunks, screened, weight, n_row, n_col)
        return jnp.concatenate(chunks, axis=0)
    phi = orbitals
    for _ in range(PASSES):
        phi = one_pass_plain(phi, screened, weight, n_row, n_col)
    return phi


def solution(mesh):
    in_specs = (P(("snap", "row", "col"), None), P("snap", "row", "col"), P("snap", None), P())
    out_specs = P(("snap", "row", "col"), None)
    return jax.shard_map(body, mesh=mesh, in_specs=in_specs, out_specs=out_specs, check_vma=False)
```

profile of v0, /device:TPU:0, one launch (start us, length us, event | category | flops | bytes accessed | tf_op | source)
XLA Modules:
  0.0 379.2 jit_solution(8721090308223268625)
XLA Ops:
  6.5 2.1 fusion.8
  8.7 4.9 %collective-permute-start.10 = (f32[128,768]{1,0:T(8,128)S(1)}, f32[128,768]{1,0:T(8,128)S(1)}, u32[]{:S(2)}, u32[]{:S(2)}) collective-permute-start(f32[128,768]{1,0:T(8,128)S(1)} %get-tuple-element.70.refs_10_), channel_id=1, source_target_pairs={{0,4},{4,8},{8,12},{1,5},{5,9},{9,13},{2,6},{6,10},{10,14},{3,7},{... | collective-permute-start | bytes 1179656 | tf_op jit(solution)/shard_map/ppermute | solution.py:189
  13.6 1.3 collective-permute-start.1
  14.9 4.6 %collective-permute-start.4 = (f32[128,768]{1,0:T(8,128)S(1)}, f32[128,768]{1,0:T(8,128)S(1)}, u32[]{:S(2)}, u32[]{:S(2)}) collective-permute-start(f32[128,768]{1,0:T(8,128)S(1)} %get-tuple-element.71.refs_3_), channel_id=1, source_target_pairs={{0,4},{4,8},{8,12},{1,5},{5,9},{9,13},{2,6},{6,10},{10,14},{3,7},{... | collective-permute-start | bytes 1179656 | tf_op jit(solution)/shard_map/ppermute | solution.py:189
  19.5 1.3 collective-permute-start.7
  20.8 2.3 collective-permute-done.10.refs_11_
  23.1 4.4 %collective-permute-start.11 = (f32[128,768]{1,0:T(8,128)S(1)}, f32[128,768]{1,0:T(8,128)S(1)}, u32[]{:S(2)}, u32[]{:S(2)}) collective-permute-start(f32[128,768]{1,0:T(8,128)S(1)} %collective-permute-done.10.refs_11_), channel_id=1, source_target_pairs={{0,4},{4,8},{8,12},{1,5},{5,9},{9,13},{2,6},{6,10},{10,14},{3,7},{... | collective-permute-start | bytes 1179656 | tf_op jit(solution)/shard_map/ppermute | solution.py:189
  28.9 2.7 collective-permute-done.4.refs_4_
  31.5 5.1 %collective-permute-start.5 = (f32[128,768]{1,0:T(8,128)S(1)}, f32[128,768]{1,0:T(8,128)}, u32[]{:S(2)}, u32[]{:S(2)}) collective-permute-start(f32[128,768]{1,0:T(8,128)S(1)} %collective-permute-done.4.refs_4_), channel_id=1, source_target_pairs={{0,4},{4,8},{8,12},{1,5},{5,9},{9,13},{2,6},{6,10},{10,14},{3,7},{... | collective-permute-start | bytes 1179656 | tf_op jit(solution)/shard_map/ppermute | solution.py:189
  36.7 1.3 collective-permute-start.8
  38.0 1.6 collective-permute-start.22
  40.0 4.4 %collective-permute-start.12 = (f32[128,768]{1,0:T(8,128)S(1)}, f32[128,768]{1,0:T(8,128)S(1)}, u32[]{:S(2)}, u32[]{:S(2)}) collective-permute-start(f32[128,768]{1,0:T(8,128)S(1)} %collective-permute-done.11.refs_12_), channel_id=1, source_target_pairs={{0,4},{4,8},{8,12},{1,5},{5,9},{9,13},{2,6},{6,10},{10,14},{3,7},{... | collective-permute-start | bytes 1179656 | tf_op jit(solution)/shard_map/ppermute | solution.py:189
  45.8 2.6 collective-permute-done.5.refs_5_
  48.4 5.2 %collective-permute-start.6 = (f32[128,768]{1,0:T(8,128)}, f32[128,768]{1,0:T(8,128)}, u32[]{:S(2)}, u32[]{:S(2)}) collective-permute-start(f32[128,768]{1,0:T(8,128)} %collective-permute-done.5.refs_5_), channel_id=1, source_target_pairs={{0,4},{4,8},{8,12},{1,5},{5,9},{9,13},{2,6},{6,10},{10,14},{3,7},{... | collective-permute-start | bytes 1179656 | tf_op jit(solution)/shard_map/ppermute | solution.py:189
  53.6 1.3 collective-permute-start.9
  54.9 1.9 collective-permute-done.12.refs_13_
  58.2 3.2 collective-permute-done.3.refs_0_
  61.4 2.8 collective-permute-done.6.refs_6_
  64.2 4.1 %collective-permute-done.9.refs_7_ = f32[128,768]{1,0:T(8,128)} collective-permute-done((f32[128,768]{1,0:T(8,128)}, f32[128,768]{1,0:T(8,128)}, u32[]{:S(2)}, u32[]{:S(2)}) %collective-permute-start.9) | collective-permute-done | bytes 393248 | tf_op jit(solution)/shard_map/ppermute | solution.py:189
  68.3 4.3 %pick.4 = (f32[128,768]{1,0:T(8,128)}, f32[128,768]{1,0:T(8,128)}, f32[128,768]{1,0:T(8,128)}, f32[128,768]{1,0:T(8,128)}, f32[128,768]{1,0:T(8,128)}, /*index=5...) custom-call(s32[4]{0:T(128)} %pad_add_fusion.1.which, ...), custom_call_target="tpu_custom_call", output_to_operand_aliasing={{0}: (15, {})} | custom-call | bytes 6291456 | tf_op jit(solution)/shard_map/pick/pallas_call | solution.py:144
  73.3 1.5 collective-permute-start.14
  78.9 1.5 collective-permute-start.20
  80.4 5.2 %collective-permute-done.14.refs_5_ = f32[128,768]{1,0:T(8,128)} collective-permute-done((f32[128,768]{1,0:T(8,128)}, f32[128,768]{1,0:T(8,128)}, u32[]{:S(2)}, u32[]{:S(2)}) %collective-permute-start.14) | collective-permute-done | bytes 393248 | tf_op jit(solution)/shard_map/ppermute | solution.py:163
  85.6 7.4 %collective-permute-done.15.refs_6_ = f32[128,768]{1,0:T(8,128)} collective-permute-done((f32[128,768]{1,0:T(8,128)}, f32[128,768]{1,0:T(8,128)}, u32[]{:S(2)}, u32[]{:S(2)}) %collective-permute-start.15) | collective-permute-done | bytes 393248 | tf_op jit(solution)/shard_map/ppermute | solution.py:163
  94.7 12.1 %apply_chunk.12.refs_1_.refs_11_ = f32[768,768]{1,0:T(8,128)S(1)} custom-call(s32[6]{0:T(128)S(1)} %copy-done.37, f32[3,768]{1,0:T(4,128)S(1)} %broadcast_multiply_fusion.refs_0_, f32[384,768]{1,0:T(8,128)S(1)} %copy-done.4, f32[384,768]{1,0:T(8,128)S(1)} %collective-permute-done.refs_2_, f32[128,768]{1,0:T(8,128)S(1)} %copy-done.21, ...), custom_call_target="tpu_custom_call" | custom-call | flops 7247757312 | bytes 11796480 | tf_op jit(solution)/shard_map/apply_chunk/pallas_call | solution.py:96
  106.8 1.4 copy-done
  109.4 12.3 %apply_chunk.13.refs_11_ = f32[768,768]{1,0:T(8,128)S(1)} custom-call(s32[6]{0:T(128)S(1)} %copy-done.35, f32[3,768]{1,0:T(4,128)S(1)} %broadcast_multiply_fusion.refs_0_, f32[384,768]{1,0:T(8,128)S(1)} %copy-done.8, f32[384,768]{1,0:T(8,128)} %collective-permute-done.23.refs_2_, f32[128,768]{1,0:T(8,128)S(1)} %copy-done.21, ...), custom_call_target="tpu_custom_call" | custom-call | flops 7247757312 | bytes 11796480 | tf_op jit(solution)/shard_map/apply_chunk/pallas_call | solution.py:96
  121.7 3.2 pick.5
  126.1 1.5 collective-permute-start.17
  130.6 12.4 %apply_chunk.14.refs_11_ = f32[768,768]{1,0:T(8,128)S(1)} custom-call(s32[6]{0:T(128)S(1)} %copy-done.33, f32[3,768]{1,0:T(4,128)S(1)} %broadcast_multiply_fusion.refs_0_, f32[384,768]{1,0:T(8,128)S(1)} %copy-done.9, f32[384,768]{1,0:T(8,128)} %collective-permute-done.23.refs_2_, f32[128,768]{1,0:T(8,128)S(1)} %copy-done.17, ...), custom_call_target="tpu_custom_call", output_to_operand_aliasing={{}: (12, {})} | custom-call | flops 7247757312 | bytes 11796480 | tf_op jit(solution)/shard_map/apply_chunk/pallas_call | solution.py:96
  143.0 1.9 collective-permute-done.18.refs_6_
  145.0 12.4 %apply_chunk.15 = f32[768,768]{1,0:T(8,128)S(1)} custom-call(s32[6]{0:T(128)S(1)} %stack.81.place, f32[3,768]{1,0:T(4,128)S(1)} %broadcast_multiply_fusion.refs_0_, f32[384,768]{1,0:T(8,128)S(1)} %copy-done.9, f32[384,768]{1,0:T(8,128)} %collective-permute-done.23.refs_2_, f32[128,768]{1,0:T(8,128)S(1)} %copy-done.22, ...), custom_call_target="tpu_custom_call", output_to_operand_aliasing={{}: (12, {})} | custom-call | flops 7247757312 | bytes 11796480 | tf_op jit(solution)/shard_map/apply_chunk/pallas_call | solution.py:96
  160.5 1.6 collective-permute-done.24
  162.1 1.4 slice_add_fusion.1.refs_12_
  163.5 1.6 collective-permute-start.26
  166.7 12.1 %apply_chunk.16.refs_11_ = f32[768,768]{1,0:T(8,128)S(1)} custom-call(s32[6]{0:T(128)S(1)} %copy-done.41, f32[3,768]{1,0:T(4,128)S(1)} %broadcast_multiply_fusion.refs_0_, f32[384,768]{1,0:T(8,128)S(1)} %copy-done.4, f32[384,768]{1,0:T(8,128)S(1)} %copy-done.6, f32[128,768]{1,0:T(8,128)S(1)} %copy-done.18, ...), custom_call_target="tpu_custom_call", output_to_operand_aliasing={{}: (12, {})} | custom-call | flops 7247757312 | bytes 11796480 | tf_op jit(solution)/shard_map/apply_chunk/pallas_call | solution.py:96
  178.8 11.9 %apply_chunk.17 = f32[768,768]{1,0:T(8,128)S(1)} custom-call(s32[6]{0:T(128)S(1)} %copy-done.39, f32[3,768]{1,0:T(4,128)S(1)} %broadcast_multiply_fusion.refs_0_, f32[384,768]{1,0:T(8,128)S(1)} %copy-done.4, f32[384,768]{1,0:T(8,128)S(1)} %copy-done.6, f32[128,768]{1,0:T(8,128)S(1)} %copy-done.23, ...), custom_call_target="tpu_custom_call", output_to_operand_aliasing={{}: (12, {})} | custom-call | flops 7247757312 | bytes 11796480 | tf_op jit(solution)/shard_map/apply_chunk/pallas_call | solution.py:96
  194.1 1.3 collective-permute-start.30
  195.4 4.6 %collective-permute-start.33 = (f32[128,768]{1,0:T(8,128)S(1)}, f32[128,768]{1,0:T(8,128)S(1)}, u32[]{:S(2)}, u32[]{:S(2)}) collective-permute-start(f32[128,768]{1,0:T(8,128)S(1)} %get-tuple-element.57.refs_3_), channel_id=1, source_target_pairs={{0,4},{4,8},{8,12},{1,5},{5,9},{9,13},{2,6},{6,10},{10,14},{3,7},{... | collective-permute-start | bytes 1179656 | tf_op jit(solution)/shard_map/ppermute | solution.py:189
  200.0 1.3 collective-permute-start.36
  201.3 4.6 %collective-permute-start.39 = (f32[128,768]{1,0:T(8,128)S(1)}, f32[128,768]{1,0:T(8,128)S(1)}, u32[]{:S(2)}, u32[]{:S(2)}) collective-permute-start(f32[128,768]{1,0:T(8,128)S(1)} %get-tuple-element.59.refs_10_), channel_id=1, source_target_pairs={{0,4},{4,8},{8,12},{1,5},{5,9},{9,13},{2,6},{6,10},{10,14},{3,7},{... | collective-permute-start | bytes 1179656 | tf_op jit(solution)/shard_map/ppermute | solution.py:189
  205.9 2.1 collective-permute-done.30.refs_2_
  209.5 4.4 %collective-permute-start.34 = (f32[128,768]{1,0:T(8,128)S(1)}, f32[128,768]{1,0:T(8,128)S(1)}, u32[]{:S(2)}, u32[]{:S(2)}) collective-permute-start(f32[128,768]{1,0:T(8,128)S(1)} %collective-permute-done.33.refs_4_), channel_id=1, source_target_pairs={{0,4},{4,8},{8,12},{1,5},{5,9},{9,13},{2,6},{6,10},{10,14},{3,7},{... | collective-permute-start | bytes 1179656 | tf_op jit(solution)/shard_map/ppermute | solution.py:189
  213.9 2.5 collective-permute-done.36.refs_9_
  217.9 4.4 %collective-permute-start.40 = (f32[128,768]{1,0:T(8,128)S(1)}, f32[128,768]{1,0:T(8,128)S(1)}, u32[]{:S(2)}, u32[]{:S(2)}) collective-permute-start(f32[128,768]{1,0:T(8,128)S(1)} %collective-permute-done.39.refs_11_), channel_id=1, source_target_pairs={{0,4},{4,8},{8,12},{1,5},{5,9},{9,13},{2,6},{6,10},{10,14},{3,7},{... | collective-permute-start | bytes 1179656 | tf_op jit(solution)/shard_map/ppermute | solution.py:189
  223.0 1.8 collective-permute-done.31.refs_1_
  226.3 4.4 %collective-permute-start.35 = (f32[128,768]{1,0:T(8,128)S(1)}, f32[128,768]{1,0:T(8,128)S(1)}, u32[]{:S(2)}, u32[]{:S(2)}) collective-permute-start(f32[128,768]{1,0:T(8,128)S(1)} %collective-permute-done.34.refs_5_), channel_id=1, source_target_pairs={{0,4},{4,8},{8,12},{1,5},{5,9},{9,13},{2,6},{6,10},{10,14},{3,7},{... | collective-permute-start | bytes 1179656 | tf_op jit(solution)/shard_map/ppermute | solution.py:189
  230.7 2.5 collective-permute-done.37.refs_8_
  234.7 5.1 %collective-permute-start.41 = (f32[128,768]{1,0:T(8,128)S(1)}, f32[128,768]{1,0:T(8,128)}, u32[]{:S(2)}, u32[]{:S(2)}) collective-permute-start(f32[128,768]{1,0:T(8,128)S(1)} %collective-permute-done.40.refs_12_), channel_id=1, source_target_pairs={{0,4},{4,8},{8,12},{1,5},{5,9},{9,13},{2,6},{6,10},{10,14},{3,7},{... | collective-permute-start | bytes 1179656 | tf_op jit(solution)/shard_map/ppermute | solution.py:189
  239.9 1.9 collective-permute-done.32.refs_0_
  243.2 6.1 %collective-permute-done.38.refs_7_ = f32[128,768]{1,0:T(8,128)S(1)} collective-permute-done((f32[128,768]{1,0:T(8,128)S(1)}, f32[128,768]{1,0:T(8,128)S(1)}, u32[]{:S(2)}, u32[]{:S(2)}) %collective-permute-start.38) | collective-permute-done | bytes 393248 | tf_op jit(solution)/shard_map/ppermute | solution.py:189
  250.5 4.2 %pick.6 = (f32[128,768]{1,0:T(8,128)}, f32[128,768]{1,0:T(8,128)}, f32[128,768]{1,0:T(8,128)}, f32[128,768]{1,0:T(8,128)}, f32[128,768]{1,0:T(8,128)}, /*index=5...) custom-call(s32[4]{0:T(128)} %pad_add_fusion.1.which, ...), custom_call_target="tpu_custom_call", output_to_operand_aliasing={{0}: (15, {})} | custom-call | bytes 6291456 | tf_op jit(solution)/shard_map/pick/pallas_call | solution.py:144
  258.7 8.9 %collective-permute-done.43.refs_5_ = f32[128,768]{1,0:T(8,128)S(1)} collective-permute-done((f32[128,768]{1,0:T(8,128)}, f32[128,768]{1,0:T(8,128)S(1)}, u32[]{:S(2)}, u32[]{:S(2)}) %collective-permute-start.43) | collective-permute-done | bytes 393248 | tf_op jit(solution)/shard_map/ppermute | solution.py:163
  267.5 6.7 %collective-permute-done.44.refs_6_ = f32[128,768]{1,0:T(8,128)S(1)} collective-permute-done((f32[128,768]{1,0:T(8,128)}, f32[128,768]{1,0:T(8,128)S(1)}, u32[]{:S(2)}, u32[]{:S(2)}) %collective-permute-start.44) | collective-permute-done | bytes 393248 | tf_op jit(solution)/shard_map/ppermute | solution.py:163
  275.8 11.5 %apply_chunk.18.refs_1_.refs_11_ = f32[768,768]{1,0:T(8,128)S(1)} custom-call(s32[6]{0:T(128)S(1)} %copy-done.38, f32[3,768]{1,0:T(4,128)S(1)} %broadcast_multiply_fusion.refs_0_, f32[384,768]{1,0:T(8,128)S(1)} %pad_maximum_fusion.refs_1_, f32[384,768]{1,0:T(8,128)S(1)} %collective-permute-done.29.refs_2_, f32[128,768]{1,0:T(8,128)S(1)} %copy-done.24, ...), custom_call_target="tpu_custom_call" | custom-call | flops 7247757312 | bytes 11796480 | tf_op jit(solution)/shard_map/apply_chunk/pallas_call | solution.py:96
  287.4 1.4 copy-done.2
  290.0 11.6 %apply_chunk.19.refs_11_ = f32[768,768]{1,0:T(8,128)S(1)} custom-call(s32[6]{0:T(128)S(1)} %copy-done.36, f32[3,768]{1,0:T(4,128)S(1)} %broadcast_multiply_fusion.refs_0_, f32[384,768]{1,0:T(8,128)S(1)} %copy-done.11, f32[384,768]{1,0:T(8,128)S(1)} %collective-permute-done.52.refs_2_, f32[128,768]{1,0:T(8,128)S(1)} %copy-done.25, ...), custom_call_target="tpu_custom_call" | custom-call | flops 7247757312 | bytes 11796480 | tf_op jit(solution)/shard_map/apply_chunk/pallas_call | solution.py:96
  302.7 3.3 pick.7
  305.9 2.1 collective-permute-start.45
  313.7 12.1 %apply_chunk.20.refs_11_ = f32[768,768]{1,0:T(8,128)S(1)} custom-call(s32[6]{0:T(128)S(1)} %copy-done.34, f32[3,768]{1,0:T(4,128)S(1)} %broadcast_multiply_fusion.refs_0_, f32[384,768]{1,0:T(8,128)S(1)} %copy-done.12, f32[384,768]{1,0:T(8,128)S(1)} %copy-done.16, f32[128,768]{1,0:T(8,128)S(1)} %copy-done.19, ...), custom_call_target="tpu_custom_call", output_to_operand_aliasing={{}: (12, {})} | custom-call | flops 7247757312 | bytes 11796480 | tf_op jit(solution)/shard_map/apply_chunk/pallas_call | solution.py:96
  326.9 11.9 %apply_chunk.21 = f32[768,768]{1,0:T(8,128)S(1)} custom-call(s32[6]{0:T(128)S(1)} %stack.81.place, f32[3,768]{1,0:T(4,128)S(1)} %broadcast_multiply_fusion.refs_0_, f32[384,768]{1,0:T(8,128)S(1)} %copy-done.12, f32[384,768]{1,0:T(8,128)S(1)} %copy-done.16, f32[128,768]{1,0:T(8,128)S(1)} %copy-done.28, ...), custom_call_target="tpu_custom_call", output_to_operand_aliasing={{}: (12, {})} | custom-call | flops 7247757312 | bytes 11796480 | tf_op jit(solution)/shard_map/apply_chunk/pallas_call | solution.py:96
  339.7 2.5 collective-permute-done.53
  342.9 12.1 %apply_chunk.22.refs_11_ = f32[768,768]{1,0:T(8,128)S(1)} custom-call(s32[6]{0:T(128)S(1)} %copy-done.42, f32[3,768]{1,0:T(4,128)S(1)} %broadcast_multiply_fusion.refs_0_, f32[384,768]{1,0:T(8,128)S(1)} %pad_maximum_fusion.refs_1_, f32[384,768]{1,0:T(8,128)S(1)} %copy-done.14, f32[128,768]{1,0:T(8,128)S(1)} %copy-done.20, ...), custom_call_target="tpu_custom_call", output_to_operand_aliasing={{}: (12, {})} | custom-call | flops 7247757312 | bytes 11796480 | tf_op jit(solution)/shard_map/apply_chunk/pallas_call | solution.py:96
  355.0 11.7 %apply_chunk.23 = f32[768,768]{1,0:T(8,128)S(1)} custom-call(s32[6]{0:T(128)S(1)} %copy-done.40, f32[3,768]{1,0:T(4,128)S(1)} %broadcast_multiply_fusion.refs_0_, f32[384,768]{1,0:T(8,128)S(1)} %pad_maximum_fusion.refs_1_, f32[384,768]{1,0:T(8,128)S(1)} %copy-done.14, f32[128,768]{1,0:T(8,128)S(1)} %copy-done.28, ...), custom_call_target="tpu_custom_call", output_to_operand_aliasing={{}: (12, {})} | custom-call | flops 7247757312 | bytes 11796480 | tf_op jit(solution)/shard_map/apply_chunk/pallas_call | solution.py:96
  (229 shorter events, 55.1 us)
Async XLA Ops:
  6.5 115.2 %all-gather.5.cloned.1.call-start = ((), (), s32[]{:S(2)}) async-start(), calls=%async_computation | async-start | bytes 1966080 | tf_op jit(solution)/shard_map/all_gather | solution.py:221
  8.7 46.2 %copy-start.49 = (f32[128,768]{1,0:T(8,128)}, f32[128,768]{1,0:T(8,128)S(1)}, u32[]{:S(2)}) copy-start(f32[128,768]{1,0:T(8,128)S(1)} %get-tuple-element.70.refs_10_) | copy-start | bytes 1179652
  8.7 48.1 %copy-start.50 = (f32[128,768]{1,0:T(8,128)}, f32[128,768]{1,0:T(8,128)S(1)}, u32[]{:S(2)}) copy-start(f32[128,768]{1,0:T(8,128)S(1)} %get-tuple-element.71.refs_3_) | copy-start | bytes 1179652
  8.7 14.4 %collective-permute-start.10 = (f32[128,768]{1,0:T(8,128)S(1)}, f32[128,768]{1,0:T(8,128)S(1)}, u32[]{:S(2)}, u32[]{:S(2)}) collective-permute-start(f32[128,768]{1,0:T(8,128)S(1)} %get-tuple-element.70.refs_10_), channel_id=1, source_target_pairs={{0,4},{4,8},{8,12},{1,5},{5,9},{9,13},{2,6},{6,10},{10,14},{3,7},{... | collective-permute-start | bytes 1179656 | tf_op jit(solution)/shard_map/ppermute | solution.py:189
  13.6 13.9 %collective-permute-start.1 = (f32[128,768]{1,0:T(8,128)S(1)}, f32[128,768]{1,0:T(8,128)S(1)}, u32[]{:S(2)}, u32[]{:S(2)}) collective-permute-start(f32[128,768]{1,0:T(8,128)S(1)} %get-tuple-element.71.refs_3_), channel_id=1, source_target_pairs={{4,0},{8,4},{12,8},{5,1},{9,5},{13,9},{6,2},{10,6},{14,10},{7,3},{... | collective-permute-start | bytes 1179656 | tf_op jit(solution)/shard_map/ppermute | solution.py:189
  14.9 16.6 %collective-permute-start.4 = (f32[128,768]{1,0:T(8,128)S(1)}, f32[128,768]{1,0:T(8,128)S(1)}, u32[]{:S(2)}, u32[]{:S(2)}) collective-permute-start(f32[128,768]{1,0:T(8,128)S(1)} %get-tuple-element.71.refs_3_), channel_id=1, source_target_pairs={{0,4},{4,8},{8,12},{1,5},{5,9},{9,13},{2,6},{6,10},{10,14},{3,7},{... | collective-permute-start | bytes 1179656 | tf_op jit(solution)/shard_map/ppermute | solution.py:189
  19.5 17.2 %collective-permute-start.7 = (f32[128,768]{1,0:T(8,128)S(1)}, f32[128,768]{1,0:T(8,128)S(1)}, u32[]{:S(2)}, u32[]{:S(2)}) collective-permute-start(f32[128,768]{1,0:T(8,128)S(1)} %get-tuple-element.70.refs_10_), channel_id=1, source_target_pairs={{4,0},{8,4},{12,8},{5,1},{9,5},{13,9},{6,2},{10,6},{14,10},{7,3},{... | collective-permute-start | bytes 1179656 | tf_op jit(solution)/shard_map/ppermute | solution.py:189
  23.1 16.9 %collective-permute-start.11 = (f32[128,768]{1,0:T(8,128)S(1)}, f32[128,768]{1,0:T(8,128)S(1)}, u32[]{:S(2)}, u32[]{:S(2)}) collective-permute-start(f32[128,768]{1,0:T(8,128)S(1)} %collective-permute-done.10.refs_11_), channel_id=1, source_target_pairs={{0,4},{4,8},{8,12},{1,5},{5,9},{9,13},{2,6},{6,10},{10,14},{3,7},{... | collective-permute-start | bytes 1179656 | tf_op jit(solution)/shard_map/ppermute | solution.py:189
  27.6 17.0 %collective-permute-start.2 = (f32[128,768]{1,0:T(8,128)S(1)}, f32[128,768]{1,0:T(8,128)}, u32[]{:S(2)}, u32[]{:S(2)}) collective-permute-start(f32[128,768]{1,0:T(8,128)S(1)} %collective-permute-done.1.refs_2_), channel_id=1, source_target_pairs={{4,0},{8,4},{12,8},{5,1},{9,5},{13,9},{6,2},{10,6},{14,10},{7,3},{... | collective-permute-start | bytes 1179656 | tf_op jit(solution)/shard_map/ppermute | solution.py:189
  31.5 16.9 %collective-permute-start.5 = (f32[128,768]{1,0:T(8,128)S(1)}, f32[128,768]{1,0:T(8,128)}, u32[]{:S(2)}, u32[]{:S(2)}) collective-permute-start(f32[128,768]{1,0:T(8,128)S(1)} %collective-permute-done.4.refs_4_), channel_id=1, source_target_pairs={{0,4},{4,8},{8,12},{1,5},{5,9},{9,13},{2,6},{6,10},{10,14},{3,7},{... | collective-permute-start | bytes 1179656 | tf_op jit(solution)/shard_map/ppermute | solution.py:189
  36.7 17.0 %collective-permute-start.8 = (f32[128,768]{1,0:T(8,128)S(1)}, f32[128,768]{1,0:T(8,128)}, u32[]{:S(2)}, u32[]{:S(2)}) collective-permute-start(f32[128,768]{1,0:T(8,128)S(1)} %collective-permute-done.7.refs_9_), channel_id=1, source_target_pairs={{4,0},{8,4},{12,8},{5,1},{9,5},{13,9},{6,2},{10,6},{14,10},{7,3},{... | collective-permute-start | bytes 1179656 | tf_op jit(solution)/shard_map/ppermute | solution.py:189
  38.0 34.7 %collective-permute-start.22 = (f32[384,768]{1,0:T(8,128)S(1)}, f32[384,768]{1,0:T(8,128)S(1)}, u32[]{:S(2)}, u32[]{:S(2)}) collective-permute-start(f32[384,768]{1,0:T(8,128)S(1)} %copy-done.4), channel_id=1, source_target_pairs={{0,2},{1,3},{2,0},{3,1},{4,6},{5,7},{6,4},{7,5},{8,10},{9,11},{10,... | collective-permute-start | bytes 3538952 | tf_op jit(solution)/shard_map/ppermute | solution.py:163
  40.0 16.9 %collective-permute-start.12 = (f32[128,768]{1,0:T(8,128)S(1)}, f32[128,768]{1,0:T(8,128)S(1)}, u32[]{:S(2)}, u32[]{:S(2)}) collective-permute-start(f32[128,768]{1,0:T(8,128)S(1)} %collective-permute-done.11.refs_12_), channel_id=1, source_target_pairs={{0,4},{4,8},{8,12},{1,5},{5,9},{9,13},{2,6},{6,10},{10,14},{3,7},{... | collective-permute-start | bytes 1179656 | tf_op jit(solution)/shard_map/ppermute | solution.py:189
  44.5 16.9 %collective-permute-start.3 = (f32[128,768]{1,0:T(8,128)}, f32[128,768]{1,0:T(8,128)}, u32[]{:S(2)}, u32[]{:S(2)}) collective-permute-start(f32[128,768]{1,0:T(8,128)} %collective-permute-done.2.refs_1_), channel_id=1, source_target_pairs={{4,0},{8,4},{12,8},{5,1},{9,5},{13,9},{6,2},{10,6},{14,10},{7,3},{... | collective-permute-start | bytes 1179656 | tf_op jit(solution)/shard_map/ppermute | solution.py:189
  48.4 15.8 %collective-permute-start.6 = (f32[128,768]{1,0:T(8,128)}, f32[128,768]{1,0:T(8,128)}, u32[]{:S(2)}, u32[]{:S(2)}) collective-permute-start(f32[128,768]{1,0:T(8,128)} %collective-permute-done.5.refs_5_), channel_id=1, source_target_pairs={{0,4},{4,8},{8,12},{1,5},{5,9},{9,13},{2,6},{6,10},{10,14},{3,7},{... | collective-permute-start | bytes 1179656 | tf_op jit(solution)/shard_map/ppermute | solution.py:189
  53.6 14.7 %collective-permute-start.9 = (f32[128,768]{1,0:T(8,128)}, f32[128,768]{1,0:T(8,128)}, u32[]{:S(2)}, u32[]{:S(2)}) collective-permute-start(f32[128,768]{1,0:T(8,128)} %collective-permute-done.8.refs_8_), channel_id=1, source_target_pairs={{4,0},{8,4},{12,8},{5,1},{9,5},{13,9},{6,2},{10,6},{14,10},{7,3},{... | collective-permute-start | bytes 1179656 | tf_op jit(solution)/shard_map/ppermute | solution.py:189
  56.8 21.3 %collective-permute-start = (f32[384,768]{1,0:T(8,128)S(1)}, f32[384,768]{1,0:T(8,128)S(1)}, u32[]{:S(2)}, u32[]{:S(2)}) collective-permute-start(f32[384,768]{1,0:T(8,128)S(1)} %copy-done.4), channel_id=1, source_target_pairs={{0,1},{1,0},{2,3},{3,2},{4,5},{5,4},{6,7},{7,6},{8,9},{9,8},{10,11... | collective-permute-start | bytes 3538952 | tf_op jit(solution)/shard_map/ppermute | solution.py:163
  72.7 230.0 %all-gather.7.cloned.1.call-start = ((), (), s32[]{:S(2)}) async-start(), calls=%async_computation.1 | async-start | bytes 1966080 | tf_op jit(solution)/shard_map/all_gather | solution.py:221
  72.7 34.0 %copy-start.7 = (f32[384,768]{1,0:T(8,128)}, f32[384,768]{1,0:T(8,128)S(1)}, u32[]{:S(2)}) copy-start(f32[384,768]{1,0:T(8,128)S(1)} %collective-permute-done.22.refs_1_) | copy-start | bytes 3538948
  72.7 35.4 %collective-permute-start.23 = (f32[384,768]{1,0:T(8,128)S(1)}, f32[384,768]{1,0:T(8,128)}, u32[]{:S(2)}, u32[]{:S(2)}) collective-permute-start(f32[384,768]{1,0:T(8,128)S(1)} %collective-permute-done.22.refs_1_), channel_id=1, source_target_pairs={{0,1},{1,0},{2,3},{3,2},{4,5},{5,4},{6,7},{7,6},{8,9},{9,8},{10,11... | collective-permute-start | bytes 3538952 | tf_op jit(solution)/shard_map/ppermute | solution.py:163
  72.8 6.1 %collective-permute-start.13 = (f32[128,768]{1,0:T(8,128)}, f32[128,768]{1,0:T(8,128)}, u32[]{:S(2)}, u32[]{:S(2)}) collective-permute-start(f32[128,768]{1,0:T(8,128)} %get-tuple-element.33), channel_id=1, source_target_pairs={{0,1},{1,0},{2,3},{3,2},{4,5},{5,4},{6,7},{7,6},{8,9},{9,8},{10,11... | collective-permute-start | bytes 1179656 | tf_op jit(solution)/shard_map/ppermute | solution.py:163
  73.3 12.3 %collective-permute-start.14 = (f32[128,768]{1,0:T(8,128)}, f32[128,768]{1,0:T(8,128)}, u32[]{:S(2)}, u32[]{:S(2)}) collective-permute-start(f32[128,768]{1,0:T(8,128)} %get-tuple-element.34), channel_id=1, source_target_pairs={{0,2},{1,3},{2,0},{3,1},{4,6},{5,7},{6,4},{7,5},{8,10},{9,11},{10,... | collective-permute-start | bytes 1179656 | tf_op jit(solution)/shard_map/ppermute | solution.py:163
  74.8 18.2 %collective-permute-start.15 = (f32[128,768]{1,0:T(8,128)}, f32[128,768]{1,0:T(8,128)}, u32[]{:S(2)}, u32[]{:S(2)}) collective-permute-start(f32[128,768]{1,0:T(8,128)} %get-tuple-element.35), channel_id=1, source_target_pairs={{0,3},{1,2},{2,1},{3,0},{4,7},{5,6},{6,5},{7,4},{8,11},{9,10},{10,... | collective-permute-start | bytes 1179656 | tf_op jit(solution)/shard_map/ppermute | solution.py:163
  78.2 49.5 %collective-permute-start.19 = (f32[128,768]{1,0:T(8,128)}, f32[128,768]{1,0:T(8,128)}, u32[]{:S(2)}, u32[]{:S(2)}) collective-permute-start(f32[128,768]{1,0:T(8,128)} %get-tuple-element.41), channel_id=1, source_target_pairs={{0,1},{1,0},{2,3},{3,2},{4,5},{5,4},{6,7},{7,6},{8,9},{9,8},{10,11... | collective-permute-start | bytes 1179656 | tf_op jit(solution)/shard_map/ppermute | solution.py:163
  78.9 48.8 %collective-permute-start.20 = (f32[128,768]{1,0:T(8,128)}, f32[128,768]{1,0:T(8,128)}, u32[]{:S(2)}, u32[]{:S(2)}) collective-permute-start(f32[128,768]{1,0:T(8,128)} %get-tuple-element.42), channel_id=1, source_target_pairs={{0,2},{1,3},{2,0},{3,1},{4,6},{5,7},{6,4},{7,5},{8,10},{9,11},{10,... | collective-permute-start | bytes 1179656 | tf_op jit(solution)/shard_map/ppermute | solution.py:163
  85.6 42.0 %collective-permute-start.21 = (f32[128,768]{1,0:T(8,128)}, f32[128,768]{1,0:T(8,128)}, u32[]{:S(2)}, u32[]{:S(2)}) collective-permute-start(f32[128,768]{1,0:T(8,128)} %get-tuple-element.43), channel_id=1, source_target_pairs={{0,3},{1,2},{2,1},{3,0},{4,7},{5,6},{6,5},{7,4},{8,11},{9,10},{10,... | collective-permute-start | bytes 1179656 | tf_op jit(solution)/shard_map/ppermute | solution.py:163
  125.0 18.0 %collective-permute-start.16 = (f32[128,768]{1,0:T(8,128)}, f32[128,768]{1,0:T(8,128)S(1)}, u32[]{:S(2)}, u32[]{:S(2)}) collective-permute-start(f32[128,768]{1,0:T(8,128)} %get-tuple-element.37), channel_id=1, source_target_pairs={{0,1},{1,0},{2,3},{3,2},{4,5},{5,4},{6,7},{7,6},{8,9},{9,8},{10,11... | collective-permute-start | bytes 1179656 | tf_op jit(solution)/shard_map/ppermute | solution.py:163
  126.1 16.9 %collective-permute-start.17 = (f32[128,768]{1,0:T(8,128)}, f32[128,768]{1,0:T(8,128)S(1)}, u32[]{:S(2)}, u32[]{:S(2)}) collective-permute-start(f32[128,768]{1,0:T(8,128)} %get-tuple-element.38), channel_id=1, source_target_pairs={{0,2},{1,3},{2,0},{3,1},{4,6},{5,7},{6,4},{7,5},{8,10},{9,11},{10,... | collective-permute-start | bytes 1179656 | tf_op jit(solution)/shard_map/ppermute | solution.py:163
  127.6 17.4 %collective-permute-start.18 = (f32[128,768]{1,0:T(8,128)}, f32[128,768]{1,0:T(8,128)S(1)}, u32[]{:S(2)}, u32[]{:S(2)}) collective-permute-start(f32[128,768]{1,0:T(8,128)} %get-tuple-element.39), channel_id=1, source_target_pairs={{0,3},{1,2},{2,1},{3,0},{4,7},{5,6},{6,5},{7,4},{8,11},{9,10},{10,... | collective-permute-start | bytes 1179656 | tf_op jit(solution)/shard_map/ppermute | solution.py:163
  158.6 3.5 collective-permute-start.24
  163.5 30.2 %collective-permute-start.26 = (f32[384,768]{1,0:T(8,128)S(1)}, f32[384,768]{1,0:T(8,128)S(1)}, u32[]{:S(2)}, u32[]{:S(2)}) collective-permute-start(f32[384,768]{1,0:T(8,128)S(1)} %slice_add_fusion.1.refs_12_), channel_id=1, source_target_pairs={{0,2},{1,3},{2,0},{3,1},{4,6},{5,7},{6,4},{7,5},{8,10},{9,11},{10,... | collective-permute-start | bytes 3538952 | tf_op jit(solution)/shard_map/ppermute | solution.py:163
  190.8 1.8 collective-permute-start.25
  190.9 2.2 collective-permute-start.27
  191.4 2.3 collective-permute-start.28
  194.1 47.7 %copy-start.45 = (f32[128,768]{1,0:T(8,128)}, f32[128,768]{1,0:T(8,128)S(1)}, u32[]{:S(2)}) copy-start(f32[128,768]{1,0:T(8,128)S(1)} %get-tuple-element.58) | copy-start | bytes 1179652
  194.1 13.9 %collective-permute-start.30 = (f32[128,768]{1,0:T(8,128)S(1)}, f32[128,768]{1,0:T(8,128)S(1)}, u32[]{:S(2)}, u32[]{:S(2)}) collective-permute-start(f32[128,768]{1,0:T(8,128)S(1)} %get-tuple-element.57.refs_3_), channel_id=1, source_target_pairs={{4,0},{8,4},{12,8},{5,1},{9,5},{13,9},{6,2},{10,6},{14,10},{7,3},{... | collective-permute-start | bytes 1179656 | tf_op jit(solution)/shard_map/ppermute | solution.py:189
  195.4 14.1 %collective-permute-start.33 = (f32[128,768]{1,0:T(8,128)S(1)}, f32[128,768]{1,0:T(8,128)S(1)}, u32[]{:S(2)}, u32[]{:S(2)}) collective-permute-start(f32[128,768]{1,0:T(8,128)S(1)} %get-tuple-element.57.refs_3_), channel_id=1, source_target_pairs={{0,4},{4,8},{8,12},{1,5},{5,9},{9,13},{2,6},{6,10},{10,14},{3,7},{... | collective-permute-start | bytes 1179656 | tf_op jit(solution)/shard_map/ppermute | solution.py:189
  200.0 16.4 %collective-permute-start.36 = (f32[128,768]{1,0:T(8,128)S(1)}, f32[128,768]{1,0:T(8,128)S(1)}, u32[]{:S(2)}, u32[]{:S(2)}) collective-permute-start(f32[128,768]{1,0:T(8,128)S(1)} %get-tuple-element.59.refs_10_), channel_id=1, source_target_pairs={{4,0},{8,4},{12,8},{5,1},{9,5},{13,9},{6,2},{10,6},{14,10},{7,3},{... | collective-permute-start | bytes 1179656 | tf_op jit(solution)/shard_map/ppermute | solution.py:189
  201.3 16.6 %collective-permute-start.39 = (f32[128,768]{1,0:T(8,128)S(1)}, f32[128,768]{1,0:T(8,128)S(1)}, u32[]{:S(2)}, u32[]{:S(2)}) collective-permute-start(f32[128,768]{1,0:T(8,128)S(1)} %get-tuple-element.59.refs_10_), channel_id=1, source_target_pairs={{0,4},{4,8},{8,12},{1,5},{5,9},{9,13},{2,6},{6,10},{10,14},{3,7},{... | collective-permute-start | bytes 1179656 | tf_op jit(solution)/shard_map/ppermute | solution.py:189
  208.0 16.9 %collective-permute-start.31 = (f32[128,768]{1,0:T(8,128)S(1)}, f32[128,768]{1,0:T(8,128)S(1)}, u32[]{:S(2)}, u32[]{:S(2)}) collective-permute-start(f32[128,768]{1,0:T(8,128)S(1)} %collective-permute-done.30.refs_2_), channel_id=1, source_target_pairs={{4,0},{8,4},{12,8},{5,1},{9,5},{13,9},{6,2},{10,6},{14,10},{7,3},{... | collective-permute-start | bytes 1179656 | tf_op jit(solution)/shard_map/ppermute | solution.py:189
  209.5 16.9 %collective-permute-start.34 = (f32[128,768]{1,0:T(8,128)S(1)}, f32[128,768]{1,0:T(8,128)S(1)}, u32[]{:S(2)}, u32[]{:S(2)}) collective-permute-start(f32[128,768]{1,0:T(8,128)S(1)} %collective-permute-done.33.refs_4_), channel_id=1, source_target_pairs={{0,4},{4,8},{8,12},{1,5},{5,9},{9,13},{2,6},{6,10},{10,14},{3,7},{... | collective-permute-start | bytes 1179656 | tf_op jit(solution)/shard_map/ppermute | solution.py:189
  216.4 16.9 %collective-permute-start.37 = (f32[128,768]{1,0:T(8,128)S(1)}, f32[128,768]{1,0:T(8,128)S(1)}, u32[]{:S(2)}, u32[]{:S(2)}) collective-permute-start(f32[128,768]{1,0:T(8,128)S(1)} %collective-permute-done.36.refs_9_), channel_id=1, source_target_pairs={{4,0},{8,4},{12,8},{5,1},{9,5},{13,9},{6,2},{10,6},{14,10},{7,3},{... | collective-permute-start | bytes 1179656 | tf_op jit(solution)/shard_map/ppermute | solution.py:189
  217.9 16.9 %collective-permute-start.40 = (f32[128,768]{1,0:T(8,128)S(1)}, f32[128,768]{1,0:T(8,128)S(1)}, u32[]{:S(2)}, u32[]{:S(2)}) collective-permute-start(f32[128,768]{1,0:T(8,128)S(1)} %collective-permute-done.39.refs_11_), channel_id=1, source_target_pairs={{0,4},{4,8},{8,12},{1,5},{5,9},{9,13},{2,6},{6,10},{10,14},{3,7},{... | collective-permute-start | bytes 1179656 | tf_op jit(solution)/shard_map/ppermute | solution.py:189
  222.4 32.3 %collective-permute-start.51 = (f32[384,768]{1,0:T(8,128)S(1)}, f32[384,768]{1,0:T(8,128)S(1)}, u32[]{:S(2)}, u32[]{:S(2)}) collective-permute-start(f32[384,768]{1,0:T(8,128)S(1)} %pad_maximum_fusion.refs_1_), channel_id=1, source_target_pairs={{0,2},{1,3},{2,0},{3,1},{4,6},{5,7},{6,4},{7,5},{8,10},{9,11},{10,... | collective-permute-start | bytes 3538952 | tf_op jit(solution)/shard_map/ppermute | solution.py:163
  224.8 17.0 %collective-permute-start.32 = (f32[128,768]{1,0:T(8,128)S(1)}, f32[128,768]{1,0:T(8,128)}, u32[]{:S(2)}, u32[]{:S(2)}) collective-permute-start(f32[128,768]{1,0:T(8,128)S(1)} %collective-permute-done.31.refs_1_), channel_id=1, source_target_pairs={{4,0},{8,4},{12,8},{5,1},{9,5},{13,9},{6,2},{10,6},{14,10},{7,3},{... | collective-permute-start | bytes 1179656 | tf_op jit(solution)/shard_map/ppermute | solution.py:189
  226.3 16.9 %collective-permute-start.35 = (f32[128,768]{1,0:T(8,128)S(1)}, f32[128,768]{1,0:T(8,128)S(1)}, u32[]{:S(2)}, u32[]{:S(2)}) collective-permute-start(f32[128,768]{1,0:T(8,128)S(1)} %collective-permute-done.34.refs_5_), channel_id=1, source_target_pairs={{0,4},{4,8},{8,12},{1,5},{5,9},{9,13},{2,6},{6,10},{10,14},{3,7},{... | collective-permute-start | bytes 1179656 | tf_op jit(solution)/shard_map/ppermute | solution.py:189
  233.2 16.0 %collective-permute-start.38 = (f32[128,768]{1,0:T(8,128)S(1)}, f32[128,768]{1,0:T(8,128)S(1)}, u32[]{:S(2)}, u32[]{:S(2)}) collective-permute-start(f32[128,768]{1,0:T(8,128)S(1)} %collective-permute-done.37.refs_8_), channel_id=1, source_target_pairs={{4,0},{8,4},{12,8},{5,1},{9,5},{13,9},{6,2},{10,6},{14,10},{7,3},{... | collective-permute-start | bytes 1179656 | tf_op jit(solution)/shard_map/ppermute | solution.py:189
  234.7 15.7 %collective-permute-start.41 = (f32[128,768]{1,0:T(8,128)S(1)}, f32[128,768]{1,0:T(8,128)}, u32[]{:S(2)}, u32[]{:S(2)}) collective-permute-start(f32[128,768]{1,0:T(8,128)S(1)} %collective-permute-done.40.refs_12_), channel_id=1, source_target_pairs={{0,4},{4,8},{8,12},{1,5},{5,9},{9,13},{2,6},{6,10},{10,14},{3,7},{... | collective-permute-start | bytes 1179656 | tf_op jit(solution)/shard_map/ppermute | solution.py:189
  241.8 15.0 %collective-permute-start.29 = (f32[384,768]{1,0:T(8,128)S(1)}, f32[384,768]{1,0:T(8,128)S(1)}, u32[]{:S(2)}, u32[]{:S(2)}) collective-permute-start(f32[384,768]{1,0:T(8,128)S(1)} %pad_maximum_fusion.refs_1_), channel_id=1, source_target_pairs={{0,1},{1,0},{2,3},{3,2},{4,5},{5,4},{6,7},{7,6},{8,9},{9,8},{10,11... | collective-permute-start | bytes 3538952 | tf_op jit(solution)/shard_map/ppermute | solution.py:163
  254.8 34.0 %collective-permute-start.52 = (f32[384,768]{1,0:T(8,128)S(1)}, f32[384,768]{1,0:T(8,128)S(1)}, u32[]{:S(2)}, u32[]{:S(2)}) collective-permute-start(f32[384,768]{1,0:T(8,128)S(1)} %collective-permute-done.51.refs_1_), channel_id=1, source_target_pairs={{0,1},{1,0},{2,3},{3,2},{4,5},{5,4},{6,7},{7,6},{8,9},{9,8},{10,11... | collective-permute-start | bytes 3538952 | tf_op jit(solution)/shard_map/ppermute | solution.py:163
  254.8 3.3 collective-permute-start.42
  255.3 12.2 %collective-permute-start.43 = (f32[128,768]{1,0:T(8,128)}, f32[128,768]{1,0:T(8,128)S(1)}, u32[]{:S(2)}, u32[]{:S(2)}) collective-permute-start(f32[128,768]{1,0:T(8,128)} %get-tuple-element.47), channel_id=1, source_target_pairs={{0,2},{1,3},{2,0},{3,1},{4,6},{5,7},{6,4},{7,5},{8,10},{9,11},{10,... | collective-permute-start | bytes 1179656 | tf_op jit(solution)/shard_map/ppermute | solution.py:163
  255.9 18.3 %collective-permute-start.44 = (f32[128,768]{1,0:T(8,128)}, f32[128,768]{1,0:T(8,128)S(1)}, u32[]{:S(2)}, u32[]{:S(2)}) collective-permute-start(f32[128,768]{1,0:T(8,128)} %get-tuple-element.48), channel_id=1, source_target_pairs={{0,3},{1,2},{2,1},{3,0},{4,7},{5,6},{6,5},{7,4},{8,11},{9,10},{10,... | collective-permute-start | bytes 1179656 | tf_op jit(solution)/shard_map/ppermute | solution.py:163
  256.8 51.7 %collective-permute-start.48 = (f32[128,768]{1,0:T(8,128)}, f32[128,768]{1,0:T(8,128)}, u32[]{:S(2)}, u32[]{:S(2)}) collective-permute-start(f32[128,768]{1,0:T(8,128)} %get-tuple-element.54), channel_id=1, source_target_pairs={{0,1},{1,0},{2,3},{3,2},{4,5},{5,4},{6,7},{7,6},{8,9},{9,8},{10,11... | collective-permute-start | bytes 1179656 | tf_op jit(solution)/shard_map/ppermute | solution.py:163
  258.1 51.3 %collective-permute-start.49 = (f32[128,768]{1,0:T(8,128)}, f32[128,768]{1,0:T(8,128)}, u32[]{:S(2)}, u32[]{:S(2)}) collective-permute-start(f32[128,768]{1,0:T(8,128)} %get-tuple-element.55), channel_id=1, source_target_pairs={{0,2},{1,3},{2,0},{3,1},{4,6},{5,7},{6,4},{7,5},{8,10},{9,11},{10,... | collective-permute-start | bytes 1179656 | tf_op jit(solution)/shard_map/ppermute | solution.py:163
  267.5 41.9 %collective-permute-start.50 = (f32[128,768]{1,0:T(8,128)}, f32[128,768]{1,0:T(8,128)}, u32[]{:S(2)}, u32[]{:S(2)}) collective-permute-start(f32[128,768]{1,0:T(8,128)} %get-tuple-element.56), channel_id=1, source_target_pairs={{0,3},{1,2},{2,1},{3,0},{4,7},{5,6},{6,5},{7,4},{8,11},{9,10},{10,... | collective-permute-start | bytes 1179656 | tf_op jit(solution)/shard_map/ppermute | solution.py:163
  305.9 19.8 %collective-permute-start.45 = (f32[128,768]{1,0:T(8,128)}, f32[128,768]{1,0:T(8,128)S(1)}, u32[]{:S(2)}, u32[]{:S(2)}) collective-permute-start(f32[128,768]{1,0:T(8,128)} %get-tuple-element.50), channel_id=1, source_target_pairs={{0,1},{1,0},{2,3},{3,2},{4,5},{5,4},{6,7},{7,6},{8,9},{9,8},{10,11... | collective-permute-start | bytes 1179656 | tf_op jit(solution)/shard_map/ppermute | solution.py:163
  308.0 17.7 %collective-permute-start.46 = (f32[128,768]{1,0:T(8,128)}, f32[128,768]{1,0:T(8,128)S(1)}, u32[]{:S(2)}, u32[]{:S(2)}) collective-permute-start(f32[128,768]{1,0:T(8,128)} %get-tuple-element.51), channel_id=1, source_target_pairs={{0,2},{1,3},{2,0},{3,1},{4,6},{5,7},{6,4},{7,5},{8,10},{9,11},{10,... | collective-permute-start | bytes 1179656 | tf_op jit(solution)/shard_map/ppermute | solution.py:163
  308.5 18.4 %collective-permute-start.47 = (f32[128,768]{1,0:T(8,128)}, f32[128,768]{1,0:T(8,128)S(1)}, u32[]{:S(2)}, u32[]{:S(2)}) collective-permute-start(f32[128,768]{1,0:T(8,128)} %get-tuple-element.52), channel_id=1, source_target_pairs={{0,3},{1,2},{2,1},{3,0},{4,7},{5,6},{6,5},{7,4},{8,11},{9,10},{10,... | collective-permute-start | bytes 1179656 | tf_op jit(solution)/shard_map/ppermute | solution.py:163
  338.9 3.2 collective-permute-start.53
  342.3 28.3 %collective-permute-start.55 = (f32[384,768]{1,0:T(8,128)S(1)}, f32[384,768]{1,0:T(8,128)S(1)}, u32[]{:S(2)}, u32[]{:S(2)}) collective-permute-start(f32[384,768]{1,0:T(8,128)S(1)} %slice_add_fusion.refs_12_), channel_id=1, source_target_pairs={{0,2},{1,3},{2,0},{3,1},{4,6},{5,7},{6,4},{7,5},{8,10},{9,11},{10,... | collective-permute-start | bytes 3538952 | tf_op jit(solution)/shard_map/ppermute | solution.py:163
  366.9 1.8 collective-permute-start.54
  367.0 2.2 collective-permute-start.56
  367.5 2.3 collective-permute-start.57
  (63 other events, 679.8 us)
Sparse Core Ops, SparseCore 0:
  72.8 37.3 all-gather.4
  254.9 38.4 all-gather.6
where the time goes:
time: 383 us; the launch traced here: 379 us
  Pallas kernels  159 us (42%)
  starting transfers between devices  92.4 us (24%)
  waiting for transfers between devices  80.4 us (21%)
  local copies, waits for them, and re-layouts  27.2 us (7%)
  between operations  14.5 us (4%)
  other arithmetic  5.55 us (1%)
    pallas_call x12, Pallas kernels, apply_chunk(): pl.pallas_call(functools.partial(apply_kernel, n, first, tiles), grid_spe...  144 us
    ppermute x24, starting transfers between devices, line_hops(): found[way * hop] = lax.ppermute(found[way * (hop - 1)], 'row', pairs)  71.6 us
    ppermute x34, waiting for transfers between devices, swap(): return lax.ppermute(value, 'col', [(i, i ^ bit) for i in range(n_col)])  41.4 us
    ppermute x24, waiting for transfers between devices, line_hops(): found[way * hop] = lax.ppermute(found[way * (hop - 1)], 'row', pairs)  39 us
    ppermute x34, starting transfers between devices, swap(): return lax.ppermute(value, 'col', [(i, i ^ bit) for i in range(n_col)])  20.7 us
    unnamed x135, local copies, waits for them, and re-layouts  20.6 us
    pallas_call x4, Pallas kernels, pick(): pl.pallas_call(functools.partial(pick_kernel, n_in, len(sets), n_on), gri...  15 us
  transfers between devices with their start and end apart: 60, of which 37 were waited for; matrix products, arithmetic and copies ran while one was open for 2% of the time, Pallas kernels for 36%

commit v1 on v0

--- a/solution.py
+++ b/solution.py
@@ -60,7 +60,7 @@
     out_ref[...] = applied if first else refs[0][...] + applied
 
 
-def apply_chunk(row_place, col_place, rows, pieces, weight, screened, partial_value, tile, after=()):
+def apply_chunk(place, row_at, col_at, rows, pieces, weight, screened, partial_value, tile, after=()):
     orbitals = rows[0].shape[1]
     n = len(pieces)
     width = pieces[0].shape[0]
@@ -69,7 +69,6 @@
     total = sum(tiles)
     n_rows = total * tile
     first = partial_value is None
-    place = jnp.stack(list(row_place) + list(col_place)).astype(jnp.int32)
     tile_spec = pl.BlockSpec((tile, orbitals), lambda i, place: (i, 0))
     in_specs = [pl.BlockSpec((times, orbitals), lambda i, place: (0, 0))]
     start = 0
@@ -83,7 +82,7 @@
         start += count
     in_specs += [pl.BlockSpec((width, orbitals), lambda i, place: (0, 0))] * n
     in_specs += [
-        pl.BlockSpec((times, tile, width), lambda i, place, p=p: (0, place[i], place[total + p]))
+        pl.BlockSpec((times, tile, width), lambda i, place, p=p: (0, place[row_at + i], place[col_at + p]))
         for p in range(n)
     ]
     args = [weight, *rows, *pieces] + [screened] * n
@@ -114,47 +113,53 @@
     )(place, *args)
 
 
-def pick_kernel(n_in, sets, n_on, which, *refs):
-    n_out = which.shape[0]
-    outs, sem = refs[len(refs) - 1 - n_out * sets : -1], refs[-1]
+def pick_kernel(n_in, sets, first, n_out, which, *refs):
+    total = n_out * sets
+    held, got, put = refs[-3:]
+    outs = refs[len(refs) - 3 - total : -3]
     for s in range(sets):
         ins = refs[s * n_in : (s + 1) * n_in]
         for p in range(n_out):
-            out, signal = outs[s * n_out + p], sem.at[s * n_out + p]
+            at = s * n_out + p
             if n_in == 1:
-                pltpu.make_async_copy(ins[0].at[which[p]], out, signal).start()
+                pltpu.make_async_copy(ins[0].at[which[first + p]], held.at[at], got.at[at]).start()
                 continue
             for j in range(n_in):
 
-                @pl.when(which[p] == j)
+                @pl.when(which[first + p] == j)
                 def _():
-                    pltpu.make_async_copy(ins[j], out, signal).start()
-
-    for p, out in enumerate(outs):
+                    pltpu.make_async_copy(ins[j], held.at[at], got.at[at]).start()
+
+    for at in range(total):
         source = refs[0].at[0] if n_in == 1 else refs[0]
-        pltpu.make_async_copy(source, out, sem.at[p]).wait()
+        pltpu.make_async_copy(source, held.at[at], got.at[at]).wait()
+        pltpu.make_async_copy(held.at[at], outs[at], put.at[at]).start()
+    for at in range(total):
+        pltpu.make_async_copy(held.at[at], outs[at], put.at[at]).wait()
 
 
 def pick(sets, which, handed=(), after=()):
-    n_in, n_out, n_on = len(sets[0]), len(which), len(handed)
+    which, first, n_out = which
+    n_in, n_on = len(sets[0]), len(handed)
     values = [value for values in sets for value in values]
     total = n_out * len(sets)
     anywhere = pl.BlockSpec(memory_space=pl.ANY)
     shape = jax.ShapeDtypeStruct(values[0].shape[-2:], values[0].dtype)
     out = pl.pallas_call(
-        functools.partial(pick_kernel, n_in, len(sets), n_on),
+        functools.partial(pick_kernel, n_in, len(sets), first, n_out),
         grid_spec=pltpu.PrefetchScalarGridSpec(
             num_scalar_prefetch=1,
             grid=(),
             in_specs=[anywhere] * (len(values) + n_on + len(after)),
-            out_specs=[anywhere] * n_on + [pl.BlockSpec(memory_space=pltpu.VMEM)] * total,
-            scratch_shapes=[pltpu.SemaphoreType.DMA((total,))],
+            out_specs=[anywhere] * (n_on + total),
+            scratch_shapes=[pltpu.VMEM((total, *shape.shape), shape.dtype)]
+            + [pltpu.SemaphoreType.DMA((total,))] * 2,
         ),
         out_shape=[shape] * (n_on + total),
         input_output_aliases={1 + len(values) + j: j for j in range(n_on)},
         cost_estimate=pl.CostEstimate(flops=0, bytes_accessed=8 * total * shape.size, transcendentals=0),
         name="pick",
-    )(jnp.stack(which).astype(jnp.int32), *values, *handed, *after)
+    )(which, *values, *handed, *after)
     picked = out[n_on:]
     return [picked[s * n_out : (s + 1) * n_out] for s in range(len(sets))], out[:n_on]
 
@@ -200,26 +205,30 @@
     there = [col_index ^ p for p in range(n_col)]
     away = [row_index - c + n_row - 1 for c in there]
     distances = range(1 - n_row, n_row)
+    place = [c * (shard // tile) + i for c in there for i in range(shard // tile)]
+    place += [c * n + k for k in range(n) for c in there]
+    place = jnp.stack(place + there + away).astype(jnp.int32)
+    there_at = len(there) * (shard // tile + n)
+    away_at = there_at + n_col
 
     found = [line_hops({0: chunk}, range(1, n_row), n_row) for chunk in chunks[:2]]
     shards = gather_relative(jnp.concatenate(chunks, axis=0), n_col)
-    picked, handed = pick([[f[d] for d in distances] for f in found], away, chunks[2:])
-
-    place = [c * (shard // tile) + i for c in there for i in range(shard // tile)]
-    cut = len(place) // 2
+    picked, handed = pick([[f[d] for d in distances] for f in found], (place, away_at, n_col), chunks[2:])
+
+    tiles = n_col * (shard // tile)
     pieces = []
 
     def apply(upper, k, partial_value, after=()):
-        col_place = [c * n + k for c in there]
         rows = shards[half:] if upper else shards[:half]
-        row_place = place[cut:] if upper else place[:cut]
-        return apply_chunk(row_place, col_place, rows, pieces[k], weight, screened, partial_value, tile, after)
+        row_at = tiles // 2 if upper else 0
+        col_at = tiles + k * n_col
+        return apply_chunk(place, row_at, col_at, rows, pieces[k], weight, screened, partial_value, tile, after)
 
     low = high = None
     for k in range(n):
         if k >= 2:
             line = lax.all_gather(handed[k - 2], "row")
-            (fetched,), _ = pick([[line]], there, (), (low,) if k == 2 else (high,))
+            (fetched,), _ = pick([[line]], (place, there_at, n_col), (), (low,) if k == 2 else (high,))
             picked.append(fetched)
         pieces.append([picked[k][0]] + [swap(picked[k][p], p, n_col) for p in range(1, n_col)])
         high = apply(True, k, high)
@@ -249,10 +258,9 @@
     piece = jnp.where(row_index == col_index // factor, piece, jnp.zeros_like(piece))
     piece = lax.psum(piece, "row")
     tile = 8 * max(d for d in range(1, 33) if rows.shape[0] % (8 * d) == 0)
-    row_place = list(jnp.arange(rows.shape[0] // tile, dtype=jnp.int32))
-    partial_value = apply_chunk(
-        row_place, [jnp.int32(0)], [rows], [piece], weight, screened, None, tile
-    )
+    tiles = rows.shape[0] // tile
+    place = jnp.arange(tiles + 1, dtype=jnp.int32) % tiles
+    partial_value = apply_chunk(place, 0, tiles, [rows], [piece], weight, screened, None, tile)
     return own - lax.psum_scatter(partial_value, "col", scatter_dimension=0, tiled=True)
 
 

time: 383 us -> 378 us (0.987)
  waiting for transfers between devices: 80.4 us -> 86.6 us
  local copies, waits for them, and re-layouts: 27.2 us -> 22 us
    unnamed x135 -> x111, local copies, waits for them, and re-layouts: 20.6 us -> 18.8 us
  transfers between devices with their start and end apart: 60 -> 60, of which waited for: 37 -> 36; matrix products, arithmetic and copies ran while one was open for 2% -> 1% of each run, Pallas kernels for 36% -> 35%
where the time goes in v1:
time: 378 us; the launch traced here: 374 us
  Pallas kernels  156 us (41%)
  starting transfers between devices  92.1 us (24%)
  waiting for transfers between devices  86.6 us (23%)
  local copies, waits for them, and re-layouts  22 us (6%)
  between operations  14.4 us (4%)
    pallas_call x12, Pallas kernels, apply_chunk(): pl.pallas_call(functools.partial(apply_kernel, n, first, tiles), grid_spe...  143 us
    ppermute x24, starting transfers between devices, line_hops(): found[way * hop] = lax.ppermute(found[way * (hop - 1)], 'row', pairs)  70.5 us
    ppermute x34, waiting for transfers between devices, swap(): return lax.ppermute(value, 'col', [(i, i ^ bit) for i in range(n_col)])  45 us
    ppermute x24, waiting for transfers between devices, line_hops(): found[way * hop] = lax.ppermute(found[way * (hop - 1)], 'row', pairs)  41.6 us
    ppermute x34, starting transfers between devices, swap(): return lax.ppermute(value, 'col', [(i, i ^ bit) for i in range(n_col)])  21.6 us
    unnamed x111, local copies, waits for them, and re-layouts  18.8 us
    pallas_call x4, Pallas kernels, pick(): pl.pallas_call(functools.partial(pick_kernel, n_in, len(sets), first, n_o...  13.2 us
  transfers between devices with their start and end apart: 60, of which 36 were waited for; matrix products, arithmetic and copies ran while one was open for 1% of the time, Pallas kernels for 35%

profile of v1, /device:TPU:0, one launch (start us, length us, event | category | flops | bytes accessed | tf_op | source)
XLA Modules:
  0.0 373.9 jit_solution(4161188346429982533)
XLA Ops:
  6.5 2.2 fusion.8
  8.7 4.9 %collective-permute-start.10 = (f32[128,768]{1,0:T(8,128)S(1)}, f32[128,768]{1,0:T(8,128)S(1)}, u32[]{:S(2)}, u32[]{:S(2)}) collective-permute-start(f32[128,768]{1,0:T(8,128)S(1)} %get-tuple-element.70.refs_10_), channel_id=1, source_target_pairs={{0,4},{4,8},{8,12},{1,5},{5,9},{9,13},{2,6},{6,10},{10,14},{3,7},{... | collective-permute-start | bytes 1179656 | tf_op jit(solution)/shard_map/ppermute | solution.py:194
  13.7 1.3 collective-permute-start.7
  15.0 4.6 %collective-permute-start.4 = (f32[128,768]{1,0:T(8,128)S(1)}, f32[128,768]{1,0:T(8,128)S(1)}, u32[]{:S(2)}, u32[]{:S(2)}) collective-permute-start(f32[128,768]{1,0:T(8,128)S(1)} %get-tuple-element.71.refs_3_), channel_id=1, source_target_pairs={{0,4},{4,8},{8,12},{1,5},{5,9},{9,13},{2,6},{6,10},{10,14},{3,7},{... | collective-permute-start | bytes 1179656 | tf_op jit(solution)/shard_map/ppermute | solution.py:194
  19.6 1.3 collective-permute-start.1
  20.9 2.3 collective-permute-done.10.refs_11_
  23.2 4.4 %collective-permute-start.11 = (f32[128,768]{1,0:T(8,128)S(1)}, f32[128,768]{1,0:T(8,128)S(1)}, u32[]{:S(2)}, u32[]{:S(2)}) collective-permute-start(f32[128,768]{1,0:T(8,128)S(1)} %collective-permute-done.10.refs_11_), channel_id=1, source_target_pairs={{0,4},{4,8},{8,12},{1,5},{5,9},{9,13},{2,6},{6,10},{10,14},{3,7},{... | collective-permute-start | bytes 1179656 | tf_op jit(solution)/shard_map/ppermute | solution.py:194
  28.9 2.7 collective-permute-done.4.refs_4_
  31.6 5.1 %collective-permute-start.5 = (f32[128,768]{1,0:T(8,128)S(1)}, f32[128,768]{1,0:T(8,128)}, u32[]{:S(2)}, u32[]{:S(2)}) collective-permute-start(f32[128,768]{1,0:T(8,128)S(1)} %collective-permute-done.4.refs_4_), channel_id=1, source_target_pairs={{0,4},{4,8},{8,12},{1,5},{5,9},{9,13},{2,6},{6,10},{10,14},{3,7},{... | collective-permute-start | bytes 1179656 | tf_op jit(solution)/shard_map/ppermute | solution.py:194
  36.7 1.3 collective-permute-start.2
  38.0 1.6 collective-permute-start.22
  40.0 4.4 %collective-permute-start.12 = (f32[128,768]{1,0:T(8,128)S(1)}, f32[128,768]{1,0:T(8,128)S(1)}, u32[]{:S(2)}, u32[]{:S(2)}) collective-permute-start(f32[128,768]{1,0:T(8,128)S(1)} %collective-permute-done.11.refs_12_), channel_id=1, source_target_pairs={{0,4},{4,8},{8,12},{1,5},{5,9},{9,13},{2,6},{6,10},{10,14},{3,7},{... | collective-permute-start | bytes 1179656 | tf_op jit(solution)/shard_map/ppermute | solution.py:194
  45.9 2.6 collective-permute-done.5.refs_5_
  48.4 5.2 %collective-permute-start.6 = (f32[128,768]{1,0:T(8,128)}, f32[128,768]{1,0:T(8,128)}, u32[]{:S(2)}, u32[]{:S(2)}) collective-permute-start(f32[128,768]{1,0:T(8,128)} %collective-permute-done.5.refs_5_), channel_id=1, source_target_pairs={{0,4},{4,8},{8,12},{1,5},{5,9},{9,13},{2,6},{6,10},{10,14},{3,7},{... | collective-permute-start | bytes 1179656 | tf_op jit(solution)/shard_map/ppermute | solution.py:194
  55.0 1.9 collective-permute-done.12.refs_13_
  58.3 3.2 collective-permute-done.9.refs_7_
  61.4 2.8 collective-permute-done.6.refs_6_
  64.3 4.1 %collective-permute-done.3.refs_0_ = f32[128,768]{1,0:T(8,128)} collective-permute-done((f32[128,768]{1,0:T(8,128)}, f32[128,768]{1,0:T(8,128)}, u32[]{:S(2)}, u32[]{:S(2)}) %collective-permute-start.3) | collective-permute-done | bytes 393248 | tf_op jit(solution)/shard_map/ppermute | solution.py:194
  68.4 3.6 pick.4
  72.7 1.5 collective-permute-start.14
  75.7 1.5 collective-permute-start.20
  77.2 7.7 %collective-permute-done.14.refs_5_ = f32[128,768]{1,0:T(8,128)S(1)} collective-permute-done((f32[128,768]{1,0:T(8,128)}, f32[128,768]{1,0:T(8,128)S(1)}, u32[]{:S(2)}, u32[]{:S(2)}) %collective-permute-start.14) | collective-permute-done | bytes 393248 | tf_op jit(solution)/shard_map/ppermute | solution.py:168
  84.9 7.5 %collective-permute-done.15.refs_6_ = f32[128,768]{1,0:T(8,128)S(1)} collective-permute-done((f32[128,768]{1,0:T(8,128)}, f32[128,768]{1,0:T(8,128)S(1)}, u32[]{:S(2)}, u32[]{:S(2)}) %collective-permute-start.15) | collective-permute-done | bytes 393248 | tf_op jit(solution)/shard_map/ppermute | solution.py:168
  93.4 11.7 %apply_chunk.12.refs_1_.refs_11_ = f32[768,768]{1,0:T(8,128)S(1)} custom-call(s32[24]{0:T(128)S(1)} %copy-done.27, f32[3,768]{1,0:T(4,128)S(1)} %broadcast_multiply_fusion.refs_0_, f32[384,768]{1,0:T(8,128)S(1)} %copy-done.4, f32[384,768]{1,0:T(8,128)S(1)} %collective-permute-done.refs_2_, f32[128,768]{1,0:T(8,128)S(1)} %copy-done.23, ...), custom_call_target="tpu_custom_call" | custom-call | flops 7247757312 | bytes 11796480 | tf_op jit(solution)/shard_map/apply_chunk/pallas_call | solution.py:95
  105.2 1.4 copy-done
  107.9 11.6 %apply_chunk.13.refs_11_ = f32[768,768]{1,0:T(8,128)S(1)} custom-call(s32[24]{0:T(128)S(1)} %copy-done.27, f32[3,768]{1,0:T(4,128)S(1)} %broadcast_multiply_fusion.refs_0_, f32[384,768]{1,0:T(8,128)S(1)} %copy-done.6, f32[384,768]{1,0:T(8,128)S(1)} %collective-permute-done.23.refs_2_, f32[128,768]{1,0:T(8,128)S(1)} %copy-done.23, ...), custom_call_target="tpu_custom_call" | custom-call | flops 7247757312 | bytes 11796480 | tf_op jit(solution)/shard_map/apply_chunk/pallas_call | solution.py:95
  120.5 3.0 pick.5
  124.6 1.5 collective-permute-start.17
  129.7 12.1 %apply_chunk.14.refs_11_ = f32[768,768]{1,0:T(8,128)S(1)} custom-call(s32[24]{0:T(128)S(1)} %copy-done.28, f32[3,768]{1,0:T(4,128)S(1)} %broadcast_multiply_fusion.refs_0_, f32[384,768]{1,0:T(8,128)S(1)} %copy-done.7, f32[384,768]{1,0:T(8,128)S(1)} %copy-done.16, f32[128,768]{1,0:T(8,128)S(1)} %copy-done.19, ...), custom_call_target="tpu_custom_call", output_to_operand_aliasing={{}: (12, {})} | custom-call | flops 7247757312 | bytes 11796480 | tf_op jit(solution)/shard_map/apply_chunk/pallas_call | solution.py:95
  141.9 1.7 collective-permute-done.18.refs_6_
  143.5 12.1 %apply_chunk.15 = f32[768,768]{1,0:T(8,128)S(1)} custom-call(s32[24]{0:T(128)S(1)} %copy-done.28, f32[3,768]{1,0:T(4,128)S(1)} %broadcast_multiply_fusion.refs_0_, f32[384,768]{1,0:T(8,128)S(1)} %copy-done.7, f32[384,768]{1,0:T(8,128)S(1)} %copy-done.16, f32[128,768]{1,0:T(8,128)S(1)} %copy-done.26, ...), custom_call_target="tpu_custom_call", output_to_operand_aliasing={{}: (12, {})} | custom-call | flops 7247757312 | bytes 11796480 | tf_op jit(solution)/shard_map/apply_chunk/pallas_call | solution.py:95
  156.5 2.5 collective-permute-done.24
  159.2 1.6 collective-permute-start.26
  160.7 12.1 %apply_chunk.16.refs_11_ = f32[768,768]{1,0:T(8,128)S(1)} custom-call(s32[24]{0:T(128)S(1)} %copy-done.28, f32[3,768]{1,0:T(4,128)S(1)} %broadcast_multiply_fusion.refs_0_, f32[384,768]{1,0:T(8,128)S(1)} %copy-done.4, f32[384,768]{1,0:T(8,128)S(1)} %copy-done.9, f32[128,768]{1,0:T(8,128)S(1)} %copy-done.20, ...), custom_call_target="tpu_custom_call", output_to_operand_aliasing={{}: (12, {})} | custom-call | flops 7247757312 | bytes 11796480 | tf_op jit(solution)/shard_map/apply_chunk/pallas_call | solution.py:95
  172.9 11.9 %apply_chunk.17 = f32[768,768]{1,0:T(8,128)S(1)} custom-call(s32[24]{0:T(128)S(1)} %copy-done.28, f32[3,768]{1,0:T(4,128)S(1)} %broadcast_multiply_fusion.refs_0_, f32[384,768]{1,0:T(8,128)S(1)} %copy-done.4, f32[384,768]{1,0:T(8,128)S(1)} %copy-done.9, f32[128,768]{1,0:T(8,128)S(1)} %copy-done.26, ...), custom_call_target="tpu_custom_call", output_to_operand_aliasing={{}: (12, {})} | custom-call | flops 7247757312 | bytes 11796480 | tf_op jit(solution)/shard_map/apply_chunk/pallas_call | solution.py:95
  188.2 3.5 collective-permute-start.33
  191.7 1.3 collective-permute-start.30
  193.0 4.6 %collective-permute-start.39 = (f32[128,768]{1,0:T(8,128)S(1)}, f32[128,768]{1,0:T(8,128)S(1)}, u32[]{:S(2)}, u32[]{:S(2)}) collective-permute-start(f32[128,768]{1,0:T(8,128)S(1)} %get-tuple-element.59.refs_10_), channel_id=1, source_target_pairs={{0,4},{4,8},{8,12},{1,5},{5,9},{9,13},{2,6},{6,10},{10,14},{3,7},{... | collective-permute-start | bytes 1179656 | tf_op jit(solution)/shard_map/ppermute | solution.py:194
  197.6 1.3 collective-permute-start.36
  198.9 2.3 collective-permute-done.33.refs_4_
  201.2 4.4 %collective-permute-start.34 = (f32[128,768]{1,0:T(8,128)S(1)}, f32[128,768]{1,0:T(8,128)S(1)}, u32[]{:S(2)}, u32[]{:S(2)}) collective-permute-start(f32[128,768]{1,0:T(8,128)S(1)} %collective-permute-done.33.refs_4_), channel_id=1, source_target_pairs={{0,4},{4,8},{8,12},{1,5},{5,9},{9,13},{2,6},{6,10},{10,14},{3,7},{... | collective-permute-start | bytes 1179656 | tf_op jit(solution)/shard_map/ppermute | solution.py:194
  206.9 2.7 collective-permute-done.39.refs_11_
  209.6 4.4 %collective-permute-start.40 = (f32[128,768]{1,0:T(8,128)S(1)}, f32[128,768]{1,0:T(8,128)S(1)}, u32[]{:S(2)}, u32[]{:S(2)}) collective-permute-start(f32[128,768]{1,0:T(8,128)S(1)} %collective-permute-done.39.refs_11_), channel_id=1, source_target_pairs={{0,4},{4,8},{8,12},{1,5},{5,9},{9,13},{2,6},{6,10},{10,14},{3,7},{... | collective-permute-start | bytes 1179656 | tf_op jit(solution)/shard_map/ppermute | solution.py:194
  218.0 5.1 %collective-permute-start.35 = (f32[128,768]{1,0:T(8,128)S(1)}, f32[128,768]{1,0:T(8,128)}, u32[]{:S(2)}, u32[]{:S(2)}) collective-permute-start(f32[128,768]{1,0:T(8,128)S(1)} %collective-permute-done.34.refs_5_), channel_id=1, source_target_pairs={{0,4},{4,8},{8,12},{1,5},{5,9},{9,13},{2,6},{6,10},{10,14},{3,7},{... | collective-permute-start | bytes 1179656 | tf_op jit(solution)/shard_map/ppermute | solution.py:194
  224.4 2.0 collective-permute-done.40.refs_12_
  226.5 4.4 %collective-permute-start.41 = (f32[128,768]{1,0:T(8,128)S(1)}, f32[128,768]{1,0:T(8,128)S(1)}, u32[]{:S(2)}, u32[]{:S(2)}) collective-permute-start(f32[128,768]{1,0:T(8,128)S(1)} %collective-permute-done.40.refs_12_), channel_id=1, source_target_pairs={{0,4},{4,8},{8,12},{1,5},{5,9},{9,13},{2,6},{6,10},{10,14},{3,7},{... | collective-permute-start | bytes 1179656 | tf_op jit(solution)/shard_map/ppermute | solution.py:194
  232.2 2.7 collective-permute-done.35.refs_6_
  235.6 3.7 collective-permute-done.32.refs_0_
  239.3 3.2 collective-permute-done.41.refs_13_
  243.3 3.5 collective-permute-done.38.refs_7_
  246.7 3.4 pick.6
  254.2 8.9 %collective-permute-done.43.refs_5_ = f32[128,768]{1,0:T(8,128)S(1)} collective-permute-done((f32[128,768]{1,0:T(8,128)}, f32[128,768]{1,0:T(8,128)S(1)}, u32[]{:S(2)}, u32[]{:S(2)}) %collective-permute-start.43) | collective-permute-done | bytes 393248 | tf_op jit(solution)/shard_map/ppermute | solution.py:168
  263.0 6.6 %collective-permute-done.44.refs_6_ = f32[128,768]{1,0:T(8,128)S(1)} collective-permute-done((f32[128,768]{1,0:T(8,128)}, f32[128,768]{1,0:T(8,128)S(1)}, u32[]{:S(2)}, u32[]{:S(2)}) %collective-permute-start.44) | collective-permute-done | bytes 393248 | tf_op jit(solution)/shard_map/ppermute | solution.py:168
  270.7 11.6 %apply_chunk.18.refs_1_.refs_11_ = f32[768,768]{1,0:T(8,128)S(1)} custom-call(s32[24]{0:T(128)S(1)} %copy-done.29, f32[3,768]{1,0:T(4,128)S(1)} %broadcast_multiply_fusion.refs_0_, f32[384,768]{1,0:T(8,128)S(1)} %pad_maximum_fusion.refs_1_, f32[384,768]{1,0:T(8,128)S(1)} %collective-permute-done.29.refs_2_, f32[128,768]{1,0:T(8,128)S(1)} %copy-done.24, ...), custom_call_target="tpu_custom_call" | custom-call | flops 7247757312 | bytes 11796480 | tf_op jit(solution)/shard_map/apply_chunk/pallas_call | solution.py:95
  282.3 1.4 copy-done.2
  285.0 11.6 %apply_chunk.19.refs_11_ = f32[768,768]{1,0:T(8,128)S(1)} custom-call(s32[24]{0:T(128)S(1)} %copy-done.29, f32[3,768]{1,0:T(4,128)S(1)} %broadcast_multiply_fusion.refs_0_, f32[384,768]{1,0:T(8,128)S(1)} %copy-done.11, f32[384,768]{1,0:T(8,128)S(1)} %collective-permute-done.52.refs_2_, f32[128,768]{1,0:T(8,128)S(1)} %copy-done.24, ...), custom_call_target="tpu_custom_call" | custom-call | flops 7247757312 | bytes 11796480 | tf_op jit(solution)/shard_map/apply_chunk/pallas_call | solution.py:95
  297.6 3.1 pick.7
  300.7 2.0 collective-permute-start.45
  307.7 12.1 %apply_chunk.20.refs_11_ = f32[768,768]{1,0:T(8,128)S(1)} custom-call(s32[24]{0:T(128)S(1)} %copy-done.30, f32[3,768]{1,0:T(4,128)S(1)} %broadcast_multiply_fusion.refs_0_, f32[384,768]{1,0:T(8,128)S(1)} %copy-done.12, f32[384,768]{1,0:T(8,128)S(1)} %copy-done.18, f32[128,768]{1,0:T(8,128)S(1)} %copy-done.21, ...), custom_call_target="tpu_custom_call", output_to_operand_aliasing={{}: (12, {})} | custom-call | flops 7247757312 | bytes 11796480 | tf_op jit(solution)/shard_map/apply_chunk/pallas_call | solution.py:95
  319.8 1.7 collective-permute-done.47.refs_6_
  321.6 11.9 %apply_chunk.21 = f32[768,768]{1,0:T(8,128)S(1)} custom-call(s32[24]{0:T(128)S(1)} %copy-done.30, f32[3,768]{1,0:T(4,128)S(1)} %broadcast_multiply_fusion.refs_0_, f32[384,768]{1,0:T(8,128)S(1)} %copy-done.12, f32[384,768]{1,0:T(8,128)S(1)} %copy-done.18, f32[128,768]{1,0:T(8,128)S(1)} %copy-done.25, ...), custom_call_target="tpu_custom_call", output_to_operand_aliasing={{}: (12, {})} | custom-call | flops 7247757312 | bytes 11796480 | tf_op jit(solution)/shard_map/apply_chunk/pallas_call | solution.py:95
  334.4 2.5 collective-permute-done.53
  337.7 12.1 %apply_chunk.22.refs_11_ = f32[768,768]{1,0:T(8,128)S(1)} custom-call(s32[24]{0:T(128)S(1)} %copy-done.30, f32[3,768]{1,0:T(4,128)S(1)} %broadcast_multiply_fusion.refs_0_, f32[384,768]{1,0:T(8,128)S(1)} %pad_maximum_fusion.refs_1_, f32[384,768]{1,0:T(8,128)S(1)} %copy-done.14, f32[128,768]{1,0:T(8,128)S(1)} %copy-done.22, ...), custom_call_target="tpu_custom_call", output_to_operand_aliasing={{}: (12, {})} | custom-call | flops 7247757312 | bytes 11796480 | tf_op jit(solution)/shard_map/apply_chunk/pallas_call | solution.py:95
  349.8 11.8 %apply_chunk.23 = f32[768,768]{1,0:T(8,128)S(1)} custom-call(s32[24]{0:T(128)S(1)} %copy-done.30, f32[3,768]{1,0:T(4,128)S(1)} %broadcast_multiply_fusion.refs_0_, f32[384,768]{1,0:T(8,128)S(1)} %pad_maximum_fusion.refs_1_, f32[384,768]{1,0:T(8,128)S(1)} %copy-done.14, f32[128,768]{1,0:T(8,128)S(1)} %copy-done.25, ...), custom_call_target="tpu_custom_call", output_to_operand_aliasing={{}: (12, {})} | custom-call | flops 7247757312 | bytes 11796480 | tf_op jit(solution)/shard_map/apply_chunk/pallas_call | solution.py:95
  (198 shorter events, 48.9 us)
Async XLA Ops:
  6.5 113.9 %all-gather.5.cloned.1.call-start = ((), (), s32[]{:S(2)}) async-start(), calls=%async_computation | async-start | bytes 1966080 | tf_op jit(solution)/shard_map/all_gather | solution.py:230
  8.7 46.2 %copy-start.37 = (f32[128,768]{1,0:T(8,128)}, f32[128,768]{1,0:T(8,128)S(1)}, u32[]{:S(2)}) copy-start(f32[128,768]{1,0:T(8,128)S(1)} %get-tuple-element.70.refs_10_) | copy-start | bytes 1179652
  8.7 48.1 %copy-start.38 = (f32[128,768]{1,0:T(8,128)}, f32[128,768]{1,0:T(8,128)S(1)}, u32[]{:S(2)}) copy-start(f32[128,768]{1,0:T(8,128)S(1)} %get-tuple-element.71.refs_3_) | copy-start | bytes 1179652
  8.7 14.4 %collective-permute-start.10 = (f32[128,768]{1,0:T(8,128)S(1)}, f32[128,768]{1,0:T(8,128)S(1)}, u32[]{:S(2)}, u32[]{:S(2)}) collective-permute-start(f32[128,768]{1,0:T(8,128)S(1)} %get-tuple-element.70.refs_10_), channel_id=1, source_target_pairs={{0,4},{4,8},{8,12},{1,5},{5,9},{9,13},{2,6},{6,10},{10,14},{3,7},{... | collective-permute-start | bytes 1179656 | tf_op jit(solution)/shard_map/ppermute | solution.py:194
  13.7 13.9 %collective-permute-start.7 = (f32[128,768]{1,0:T(8,128)S(1)}, f32[128,768]{1,0:T(8,128)S(1)}, u32[]{:S(2)}, u32[]{:S(2)}) collective-permute-start(f32[128,768]{1,0:T(8,128)S(1)} %get-tuple-element.70.refs_10_), channel_id=1, source_target_pairs={{4,0},{8,4},{12,8},{5,1},{9,5},{13,9},{6,2},{10,6},{14,10},{7,3},{... | collective-permute-start | bytes 1179656 | tf_op jit(solution)/shard_map/ppermute | solution.py:194
  15.0 16.6 %collective-permute-start.4 = (f32[128,768]{1,0:T(8,128)S(1)}, f32[128,768]{1,0:T(8,128)S(1)}, u32[]{:S(2)}, u32[]{:S(2)}) collective-permute-start(f32[128,768]{1,0:T(8,128)S(1)} %get-tuple-element.71.refs_3_), channel_id=1, source_target_pairs={{0,4},{4,8},{8,12},{1,5},{5,9},{9,13},{2,6},{6,10},{10,14},{3,7},{... | collective-permute-start | bytes 1179656 | tf_op jit(solution)/shard_map/ppermute | solution.py:194
  19.6 17.2 %collective-permute-start.1 = (f32[128,768]{1,0:T(8,128)S(1)}, f32[128,768]{1,0:T(8,128)S(1)}, u32[]{:S(2)}, u32[]{:S(2)}) collective-permute-start(f32[128,768]{1,0:T(8,128)S(1)} %get-tuple-element.71.refs_3_), channel_id=1, source_target_pairs={{4,0},{8,4},{12,8},{5,1},{9,5},{13,9},{6,2},{10,6},{14,10},{7,3},{... | collective-permute-start | bytes 1179656 | tf_op jit(solution)/shard_map/ppermute | solution.py:194
  23.2 16.9 %collective-permute-start.11 = (f32[128,768]{1,0:T(8,128)S(1)}, f32[128,768]{1,0:T(8,128)S(1)}, u32[]{:S(2)}, u32[]{:S(2)}) collective-permute-start(f32[128,768]{1,0:T(8,128)S(1)} %collective-permute-done.10.refs_11_), channel_id=1, source_target_pairs={{0,4},{4,8},{8,12},{1,5},{5,9},{9,13},{2,6},{6,10},{10,14},{3,7},{... | collective-permute-start | bytes 1179656 | tf_op jit(solution)/shard_map/ppermute | solution.py:194
  27.6 17.0 %collective-permute-start.8 = (f32[128,768]{1,0:T(8,128)S(1)}, f32[128,768]{1,0:T(8,128)}, u32[]{:S(2)}, u32[]{:S(2)}) collective-permute-start(f32[128,768]{1,0:T(8,128)S(1)} %collective-permute-done.7.refs_9_), channel_id=1, source_target_pairs={{4,0},{8,4},{12,8},{5,1},{9,5},{13,9},{6,2},{10,6},{14,10},{7,3},{... | collective-permute-start | bytes 1179656 | tf_op jit(solution)/shard_map/ppermute | solution.py:194
  31.6 16.9 %collective-permute-start.5 = (f32[128,768]{1,0:T(8,128)S(1)}, f32[128,768]{1,0:T(8,128)}, u32[]{:S(2)}, u32[]{:S(2)}) collective-permute-start(f32[128,768]{1,0:T(8,128)S(1)} %collective-permute-done.4.refs_4_), channel_id=1, source_target_pairs={{0,4},{4,8},{8,12},{1,5},{5,9},{9,13},{2,6},{6,10},{10,14},{3,7},{... | collective-permute-start | bytes 1179656 | tf_op jit(solution)/shard_map/ppermute | solution.py:194
  36.7 17.0 %collective-permute-start.2 = (f32[128,768]{1,0:T(8,128)S(1)}, f32[128,768]{1,0:T(8,128)}, u32[]{:S(2)}, u32[]{:S(2)}) collective-permute-start(f32[128,768]{1,0:T(8,128)S(1)} %collective-permute-done.1.refs_2_), channel_id=1, source_target_pairs={{4,0},{8,4},{12,8},{5,1},{9,5},{13,9},{6,2},{10,6},{14,10},{7,3},{... | collective-permute-start | bytes 1179656 | tf_op jit(solution)/shard_map/ppermute | solution.py:194
  38.0 34.1 %collective-permute-start.22 = (f32[384,768]{1,0:T(8,128)S(1)}, f32[384,768]{1,0:T(8,128)S(1)}, u32[]{:S(2)}, u32[]{:S(2)}) collective-permute-start(f32[384,768]{1,0:T(8,128)S(1)} %copy-done.4), channel_id=1, source_target_pairs={{0,2},{1,3},{2,0},{3,1},{4,6},{5,7},{6,4},{7,5},{8,10},{9,11},{10,... | collective-permute-start | bytes 3538952 | tf_op jit(solution)/shard_map/ppermute | solution.py:168
  40.0 16.9 %collective-permute-start.12 = (f32[128,768]{1,0:T(8,128)S(1)}, f32[128,768]{1,0:T(8,128)S(1)}, u32[]{:S(2)}, u32[]{:S(2)}) collective-permute-start(f32[128,768]{1,0:T(8,128)S(1)} %collective-permute-done.11.refs_12_), channel_id=1, source_target_pairs={{0,4},{4,8},{8,12},{1,5},{5,9},{9,13},{2,6},{6,10},{10,14},{3,7},{... | collective-permute-start | bytes 1179656 | tf_op jit(solution)/shard_map/ppermute | solution.py:194
  44.6 16.9 %collective-permute-start.9 = (f32[128,768]{1,0:T(8,128)}, f32[128,768]{1,0:T(8,128)}, u32[]{:S(2)}, u32[]{:S(2)}) collective-permute-start(f32[128,768]{1,0:T(8,128)} %collective-permute-done.8.refs_8_), channel_id=1, source_target_pairs={{4,0},{8,4},{12,8},{5,1},{9,5},{13,9},{6,2},{10,6},{14,10},{7,3},{... | collective-permute-start | bytes 1179656 | tf_op jit(solution)/shard_map/ppermute | solution.py:194
  48.4 15.8 %collective-permute-start.6 = (f32[128,768]{1,0:T(8,128)}, f32[128,768]{1,0:T(8,128)}, u32[]{:S(2)}, u32[]{:S(2)}) collective-permute-start(f32[128,768]{1,0:T(8,128)} %collective-permute-done.5.refs_5_), channel_id=1, source_target_pairs={{0,4},{4,8},{8,12},{1,5},{5,9},{9,13},{2,6},{6,10},{10,14},{3,7},{... | collective-permute-start | bytes 1179656 | tf_op jit(solution)/shard_map/ppermute | solution.py:194
  53.7 14.7 %collective-permute-start.3 = (f32[128,768]{1,0:T(8,128)}, f32[128,768]{1,0:T(8,128)}, u32[]{:S(2)}, u32[]{:S(2)}) collective-permute-start(f32[128,768]{1,0:T(8,128)} %collective-permute-done.2.refs_1_), channel_id=1, source_target_pairs={{4,0},{8,4},{12,8},{5,1},{9,5},{13,9},{6,2},{10,6},{14,10},{7,3},{... | collective-permute-start | bytes 1179656 | tf_op jit(solution)/shard_map/ppermute | solution.py:194
  56.9 18.1 %collective-permute-start = (f32[384,768]{1,0:T(8,128)S(1)}, f32[384,768]{1,0:T(8,128)S(1)}, u32[]{:S(2)}, u32[]{:S(2)}) collective-permute-start(f32[384,768]{1,0:T(8,128)S(1)} %copy-done.4), channel_id=1, source_target_pairs={{0,1},{1,0},{2,3},{3,2},{4,5},{5,4},{6,7},{7,6},{8,9},{9,8},{10,11... | collective-permute-start | bytes 3538952 | tf_op jit(solution)/shard_map/ppermute | solution.py:168
  72.0 225.5 %all-gather.7.cloned.1.call-start = ((), (), s32[]{:S(2)}) async-start(), calls=%async_computation.1 | async-start | bytes 1966080 | tf_op jit(solution)/shard_map/all_gather | solution.py:230
  72.1 34.5 %collective-permute-start.23 = (f32[384,768]{1,0:T(8,128)S(1)}, f32[384,768]{1,0:T(8,128)S(1)}, u32[]{:S(2)}, u32[]{:S(2)}) collective-permute-start(f32[384,768]{1,0:T(8,128)S(1)} %collective-permute-done.22.refs_1_), channel_id=1, source_target_pairs={{0,1},{1,0},{2,3},{3,2},{4,5},{5,4},{6,7},{7,6},{8,9},{9,8},{10,11... | collective-permute-start | bytes 3538952 | tf_op jit(solution)/shard_map/ppermute | solution.py:168
  72.2 3.5 collective-permute-start.13
  72.7 12.2 %collective-permute-start.14 = (f32[128,768]{1,0:T(8,128)}, f32[128,768]{1,0:T(8,128)S(1)}, u32[]{:S(2)}, u32[]{:S(2)}) collective-permute-start(f32[128,768]{1,0:T(8,128)} %get-tuple-element.34), channel_id=1, source_target_pairs={{0,2},{1,3},{2,0},{3,1},{4,6},{5,7},{6,4},{7,5},{8,10},{9,11},{10,... | collective-permute-start | bytes 1179656 | tf_op jit(solution)/shard_map/ppermute | solution.py:168
  74.2 18.2 %collective-permute-start.15 = (f32[128,768]{1,0:T(8,128)}, f32[128,768]{1,0:T(8,128)S(1)}, u32[]{:S(2)}, u32[]{:S(2)}) collective-permute-start(f32[128,768]{1,0:T(8,128)} %get-tuple-element.35), channel_id=1, source_target_pairs={{0,3},{1,2},{2,1},{3,0},{4,7},{5,6},{6,5},{7,4},{8,11},{9,10},{10,... | collective-permute-start | bytes 1179656 | tf_op jit(solution)/shard_map/ppermute | solution.py:168
  75.0 51.2 %collective-permute-start.19 = (f32[128,768]{1,0:T(8,128)}, f32[128,768]{1,0:T(8,128)}, u32[]{:S(2)}, u32[]{:S(2)}) collective-permute-start(f32[128,768]{1,0:T(8,128)} %get-tuple-element.41), channel_id=1, source_target_pairs={{0,1},{1,0},{2,3},{3,2},{4,5},{5,4},{6,7},{7,6},{8,9},{9,8},{10,11... | collective-permute-start | bytes 1179656 | tf_op jit(solution)/shard_map/ppermute | solution.py:168
  75.7 50.5 %collective-permute-start.20 = (f32[128,768]{1,0:T(8,128)}, f32[128,768]{1,0:T(8,128)}, u32[]{:S(2)}, u32[]{:S(2)}) collective-permute-start(f32[128,768]{1,0:T(8,128)} %get-tuple-element.42), channel_id=1, source_target_pairs={{0,2},{1,3},{2,0},{3,1},{4,6},{5,7},{6,4},{7,5},{8,10},{9,11},{10,... | collective-permute-start | bytes 1179656 | tf_op jit(solution)/shard_map/ppermute | solution.py:168
  84.9 41.3 %collective-permute-start.21 = (f32[128,768]{1,0:T(8,128)}, f32[128,768]{1,0:T(8,128)}, u32[]{:S(2)}, u32[]{:S(2)}) collective-permute-start(f32[128,768]{1,0:T(8,128)} %get-tuple-element.43), channel_id=1, source_target_pairs={{0,3},{1,2},{2,1},{3,0},{4,7},{5,6},{6,5},{7,4},{8,11},{9,10},{10,... | collective-permute-start | bytes 1179656 | tf_op jit(solution)/shard_map/ppermute | solution.py:168
  123.5 18.4 %collective-permute-start.16 = (f32[128,768]{1,0:T(8,128)}, f32[128,768]{1,0:T(8,128)S(1)}, u32[]{:S(2)}, u32[]{:S(2)}) collective-permute-start(f32[128,768]{1,0:T(8,128)} %get-tuple-element.37), channel_id=1, source_target_pairs={{0,1},{1,0},{2,3},{3,2},{4,5},{5,4},{6,7},{7,6},{8,9},{9,8},{10,11... | collective-permute-start | bytes 1179656 | tf_op jit(solution)/shard_map/ppermute | solution.py:168
  124.6 17.2 %collective-permute-start.17 = (f32[128,768]{1,0:T(8,128)}, f32[128,768]{1,0:T(8,128)S(1)}, u32[]{:S(2)}, u32[]{:S(2)}) collective-permute-start(f32[128,768]{1,0:T(8,128)} %get-tuple-element.38), channel_id=1, source_target_pairs={{0,2},{1,3},{2,0},{3,1},{4,6},{5,7},{6,4},{7,5},{8,10},{9,11},{10,... | collective-permute-start | bytes 1179656 | tf_op jit(solution)/shard_map/ppermute | solution.py:168
  126.1 17.4 %collective-permute-start.18 = (f32[128,768]{1,0:T(8,128)}, f32[128,768]{1,0:T(8,128)S(1)}, u32[]{:S(2)}, u32[]{:S(2)}) collective-permute-start(f32[128,768]{1,0:T(8,128)} %get-tuple-element.39), channel_id=1, source_target_pairs={{0,3},{1,2},{2,1},{3,0},{4,7},{5,6},{6,5},{7,4},{8,11},{9,10},{10,... | collective-permute-start | bytes 1179656 | tf_op jit(solution)/shard_map/ppermute | solution.py:168
  155.8 3.2 collective-permute-start.24
  159.2 28.7 %collective-permute-start.26 = (f32[384,768]{1,0:T(8,128)S(1)}, f32[384,768]{1,0:T(8,128)S(1)}, u32[]{:S(2)}, u32[]{:S(2)}) collective-permute-start(f32[384,768]{1,0:T(8,128)S(1)} %slice_add_fusion.1.refs_12_), channel_id=1, source_target_pairs={{0,2},{1,3},{2,0},{3,1},{4,6},{5,7},{6,4},{7,5},{8,10},{9,11},{10,... | collective-permute-start | bytes 3538952 | tf_op jit(solution)/shard_map/ppermute | solution.py:168
  184.9 1.8 collective-permute-start.25
  185.1 2.2 collective-permute-start.28
  185.5 2.3 collective-permute-start.27
  188.2 46.7 %copy-start.33 = (f32[128,768]{1,0:T(8,128)}, f32[128,768]{1,0:T(8,128)S(1)}, u32[]{:S(2)}) copy-start(f32[128,768]{1,0:T(8,128)S(1)} %get-tuple-element.58) | copy-start | bytes 1179652
  188.2 13.0 %collective-permute-start.33 = (f32[128,768]{1,0:T(8,128)S(1)}, f32[128,768]{1,0:T(8,128)S(1)}, u32[]{:S(2)}, u32[]{:S(2)}) collective-permute-start(f32[128,768]{1,0:T(8,128)S(1)} %get-tuple-element.57.refs_3_), channel_id=1, source_target_pairs={{0,4},{4,8},{8,12},{1,5},{5,9},{9,13},{2,6},{6,10},{10,14},{3,7},{... | collective-permute-start | bytes 1179656 | tf_op jit(solution)/shard_map/ppermute | solution.py:194
  191.7 13.9 %collective-permute-start.30 = (f32[128,768]{1,0:T(8,128)S(1)}, f32[128,768]{1,0:T(8,128)S(1)}, u32[]{:S(2)}, u32[]{:S(2)}) collective-permute-start(f32[128,768]{1,0:T(8,128)S(1)} %get-tuple-element.57.refs_3_), channel_id=1, source_target_pairs={{4,0},{8,4},{12,8},{5,1},{9,5},{13,9},{6,2},{10,6},{14,10},{7,3},{... | collective-permute-start | bytes 1179656 | tf_op jit(solution)/shard_map/ppermute | solution.py:194
  193.0 16.6 %collective-permute-start.39 = (f32[128,768]{1,0:T(8,128)S(1)}, f32[128,768]{1,0:T(8,128)S(1)}, u32[]{:S(2)}, u32[]{:S(2)}) collective-permute-start(f32[128,768]{1,0:T(8,128)S(1)} %get-tuple-element.59.refs_10_), channel_id=1, source_target_pairs={{0,4},{4,8},{8,12},{1,5},{5,9},{9,13},{2,6},{6,10},{10,14},{3,7},{... | collective-permute-start | bytes 1179656 | tf_op jit(solution)/shard_map/ppermute | solution.py:194
  197.6 16.4 %collective-permute-start.36 = (f32[128,768]{1,0:T(8,128)S(1)}, f32[128,768]{1,0:T(8,128)S(1)}, u32[]{:S(2)}, u32[]{:S(2)}) collective-permute-start(f32[128,768]{1,0:T(8,128)S(1)} %get-tuple-element.59.refs_10_), channel_id=1, source_target_pairs={{4,0},{8,4},{12,8},{5,1},{9,5},{13,9},{6,2},{10,6},{14,10},{7,3},{... | collective-permute-start | bytes 1179656 | tf_op jit(solution)/shard_map/ppermute | solution.py:194
  201.2 16.9 %collective-permute-start.34 = (f32[128,768]{1,0:T(8,128)S(1)}, f32[128,768]{1,0:T(8,128)S(1)}, u32[]{:S(2)}, u32[]{:S(2)}) collective-permute-start(f32[128,768]{1,0:T(8,128)S(1)} %collective-permute-done.33.refs_4_), channel_id=1, source_target_pairs={{0,4},{4,8},{8,12},{1,5},{5,9},{9,13},{2,6},{6,10},{10,14},{3,7},{... | collective-permute-start | bytes 1179656 | tf_op jit(solution)/shard_map/ppermute | solution.py:194
  205.6 17.5 %collective-permute-start.31 = (f32[128,768]{1,0:T(8,128)S(1)}, f32[128,768]{1,0:T(8,128)S(1)}, u32[]{:S(2)}, u32[]{:S(2)}) collective-permute-start(f32[128,768]{1,0:T(8,128)S(1)} %collective-permute-done.30.refs_2_), channel_id=1, source_target_pairs={{4,0},{8,4},{12,8},{5,1},{9,5},{13,9},{6,2},{10,6},{14,10},{7,3},{... | collective-permute-start | bytes 1179656 | tf_op jit(solution)/shard_map/ppermute | solution.py:194
  209.6 16.9 %collective-permute-start.40 = (f32[128,768]{1,0:T(8,128)S(1)}, f32[128,768]{1,0:T(8,128)S(1)}, u32[]{:S(2)}, u32[]{:S(2)}) collective-permute-start(f32[128,768]{1,0:T(8,128)S(1)} %collective-permute-done.39.refs_11_), channel_id=1, source_target_pairs={{0,4},{4,8},{8,12},{1,5},{5,9},{9,13},{2,6},{6,10},{10,14},{3,7},{... | collective-permute-start | bytes 1179656 | tf_op jit(solution)/shard_map/ppermute | solution.py:194
  214.1 16.9 %collective-permute-start.37 = (f32[128,768]{1,0:T(8,128)S(1)}, f32[128,768]{1,0:T(8,128)S(1)}, u32[]{:S(2)}, u32[]{:S(2)}) collective-permute-start(f32[128,768]{1,0:T(8,128)S(1)} %collective-permute-done.36.refs_9_), channel_id=1, source_target_pairs={{4,0},{8,4},{12,8},{5,1},{9,5},{13,9},{6,2},{10,6},{14,10},{7,3},{... | collective-permute-start | bytes 1179656 | tf_op jit(solution)/shard_map/ppermute | solution.py:194
  215.5 34.7 %collective-permute-start.51 = (f32[384,768]{1,0:T(8,128)S(1)}, f32[384,768]{1,0:T(8,128)S(1)}, u32[]{:S(2)}, u32[]{:S(2)}) collective-permute-start(f32[384,768]{1,0:T(8,128)S(1)} %pad_maximum_fusion.refs_1_), channel_id=1, source_target_pairs={{0,2},{1,3},{2,0},{3,1},{4,6},{5,7},{6,4},{7,5},{8,10},{9,11},{10,... | collective-permute-start | bytes 3538952 | tf_op jit(solution)/shard_map/ppermute | solution.py:168
  218.0 16.9 %collective-permute-start.35 = (f32[128,768]{1,0:T(8,128)S(1)}, f32[128,768]{1,0:T(8,128)}, u32[]{:S(2)}, u32[]{:S(2)}) collective-permute-start(f32[128,768]{1,0:T(8,128)S(1)} %collective-permute-done.34.refs_5_), channel_id=1, source_target_pairs={{0,4},{4,8},{8,12},{1,5},{5,9},{9,13},{2,6},{6,10},{10,14},{3,7},{... | collective-permute-start | bytes 1179656 | tf_op jit(solution)/shard_map/ppermute | solution.py:194
  223.2 16.2 %collective-permute-start.32 = (f32[128,768]{1,0:T(8,128)S(1)}, f32[128,768]{1,0:T(8,128)S(1)}, u32[]{:S(2)}, u32[]{:S(2)}) collective-permute-start(f32[128,768]{1,0:T(8,128)S(1)} %collective-permute-done.31.refs_1_), channel_id=1, source_target_pairs={{4,0},{8,4},{12,8},{5,1},{9,5},{13,9},{6,2},{10,6},{14,10},{7,3},{... | collective-permute-start | bytes 1179656 | tf_op jit(solution)/shard_map/ppermute | solution.py:194
  226.5 16.0 %collective-permute-start.41 = (f32[128,768]{1,0:T(8,128)S(1)}, f32[128,768]{1,0:T(8,128)S(1)}, u32[]{:S(2)}, u32[]{:S(2)}) collective-permute-start(f32[128,768]{1,0:T(8,128)S(1)} %collective-permute-done.40.refs_12_), channel_id=1, source_target_pairs={{0,4},{4,8},{8,12},{1,5},{5,9},{9,13},{2,6},{6,10},{10,14},{3,7},{... | collective-permute-start | bytes 1179656 | tf_op jit(solution)/shard_map/ppermute | solution.py:194
  230.9 15.8 %collective-permute-start.38 = (f32[128,768]{1,0:T(8,128)S(1)}, f32[128,768]{1,0:T(8,128)}, u32[]{:S(2)}, u32[]{:S(2)}) collective-permute-start(f32[128,768]{1,0:T(8,128)S(1)} %collective-permute-done.37.refs_8_), channel_id=1, source_target_pairs={{4,0},{8,4},{12,8},{5,1},{9,5},{13,9},{6,2},{10,6},{14,10},{7,3},{... | collective-permute-start | bytes 1179656 | tf_op jit(solution)/shard_map/ppermute | solution.py:194
  234.9 17.4 %collective-permute-start.29 = (f32[384,768]{1,0:T(8,128)S(1)}, f32[384,768]{1,0:T(8,128)S(1)}, u32[]{:S(2)}, u32[]{:S(2)}) collective-permute-start(f32[384,768]{1,0:T(8,128)S(1)} %pad_maximum_fusion.refs_1_), channel_id=1, source_target_pairs={{0,1},{1,0},{2,3},{3,2},{4,5},{5,4},{6,7},{7,6},{8,9},{9,8},{10,11... | collective-permute-start | bytes 3538952 | tf_op jit(solution)/shard_map/ppermute | solution.py:168
  235.6 34.0 %copy-start.29 = (s32[24]{0:T(128)S(1)}, s32[24]{0:T(128)}, u32[]{:S(2)}) copy-start(s32[24]{0:T(128)} %stack.112.which.place) | copy-start | bytes 292
  250.2 33.4 %collective-permute-start.52 = (f32[384,768]{1,0:T(8,128)S(1)}, f32[384,768]{1,0:T(8,128)S(1)}, u32[]{:S(2)}, u32[]{:S(2)}) collective-permute-start(f32[384,768]{1,0:T(8,128)S(1)} %collective-permute-done.51.refs_1_), channel_id=1, source_target_pairs={{0,1},{1,0},{2,3},{3,2},{4,5},{5,4},{6,7},{7,6},{8,9},{9,8},{10,11... | collective-permute-start | bytes 3538952 | tf_op jit(solution)/shard_map/ppermute | solution.py:168
  250.3 3.3 collective-permute-start.42
  250.8 12.2 %collective-permute-start.43 = (f32[128,768]{1,0:T(8,128)}, f32[128,768]{1,0:T(8,128)S(1)}, u32[]{:S(2)}, u32[]{:S(2)}) collective-permute-start(f32[128,768]{1,0:T(8,128)} %get-tuple-element.47), channel_id=1, source_target_pairs={{0,2},{1,3},{2,0},{3,1},{4,6},{5,7},{6,4},{7,5},{8,10},{9,11},{10,... | collective-permute-start | bytes 1179656 | tf_op jit(solution)/shard_map/ppermute | solution.py:168
  251.4 18.3 %collective-permute-start.44 = (f32[128,768]{1,0:T(8,128)}, f32[128,768]{1,0:T(8,128)S(1)}, u32[]{:S(2)}, u32[]{:S(2)}) collective-permute-start(f32[128,768]{1,0:T(8,128)} %get-tuple-element.48), channel_id=1, source_target_pairs={{0,3},{1,2},{2,1},{3,0},{4,7},{5,6},{6,5},{7,4},{8,11},{9,10},{10,... | collective-permute-start | bytes 1179656 | tf_op jit(solution)/shard_map/ppermute | solution.py:168
  252.3 51.0 %collective-permute-start.48 = (f32[128,768]{1,0:T(8,128)}, f32[128,768]{1,0:T(8,128)}, u32[]{:S(2)}, u32[]{:S(2)}) collective-permute-start(f32[128,768]{1,0:T(8,128)} %get-tuple-element.54), channel_id=1, source_target_pairs={{0,1},{1,0},{2,3},{3,2},{4,5},{5,4},{6,7},{7,6},{8,9},{9,8},{10,11... | collective-permute-start | bytes 1179656 | tf_op jit(solution)/shard_map/ppermute | solution.py:168
  253.6 50.6 %collective-permute-start.49 = (f32[128,768]{1,0:T(8,128)}, f32[128,768]{1,0:T(8,128)}, u32[]{:S(2)}, u32[]{:S(2)}) collective-permute-start(f32[128,768]{1,0:T(8,128)} %get-tuple-element.55), channel_id=1, source_target_pairs={{0,2},{1,3},{2,0},{3,1},{4,6},{5,7},{6,4},{7,5},{8,10},{9,11},{10,... | collective-permute-start | bytes 1179656 | tf_op jit(solution)/shard_map/ppermute | solution.py:168
  263.0 41.1 %collective-permute-start.50 = (f32[128,768]{1,0:T(8,128)}, f32[128,768]{1,0:T(8,128)}, u32[]{:S(2)}, u32[]{:S(2)}) collective-permute-start(f32[128,768]{1,0:T(8,128)} %get-tuple-element.56), channel_id=1, source_target_pairs={{0,3},{1,2},{2,1},{3,0},{4,7},{5,6},{6,5},{7,4},{8,11},{9,10},{10,... | collective-permute-start | bytes 1179656 | tf_op jit(solution)/shard_map/ppermute | solution.py:168
  300.7 19.2 %collective-permute-start.45 = (f32[128,768]{1,0:T(8,128)}, f32[128,768]{1,0:T(8,128)S(1)}, u32[]{:S(2)}, u32[]{:S(2)}) collective-permute-start(f32[128,768]{1,0:T(8,128)} %get-tuple-element.50), channel_id=1, source_target_pairs={{0,1},{1,0},{2,3},{3,2},{4,5},{5,4},{6,7},{7,6},{8,9},{9,8},{10,11... | collective-permute-start | bytes 1179656 | tf_op jit(solution)/shard_map/ppermute | solution.py:168
  302.7 17.1 %collective-permute-start.46 = (f32[128,768]{1,0:T(8,128)}, f32[128,768]{1,0:T(8,128)S(1)}, u32[]{:S(2)}, u32[]{:S(2)}) collective-permute-start(f32[128,768]{1,0:T(8,128)} %get-tuple-element.51), channel_id=1, source_target_pairs={{0,2},{1,3},{2,0},{3,1},{4,6},{5,7},{6,4},{7,5},{8,10},{9,11},{10,... | collective-permute-start | bytes 1179656 | tf_op jit(solution)/shard_map/ppermute | solution.py:168
  303.3 18.3 %collective-permute-start.47 = (f32[128,768]{1,0:T(8,128)}, f32[128,768]{1,0:T(8,128)S(1)}, u32[]{:S(2)}, u32[]{:S(2)}) collective-permute-start(f32[128,768]{1,0:T(8,128)} %get-tuple-element.52), channel_id=1, source_target_pairs={{0,3},{1,2},{2,1},{3,0},{4,7},{5,6},{6,5},{7,4},{8,11},{9,10},{10,... | collective-permute-start | bytes 1179656 | tf_op jit(solution)/shard_map/ppermute | solution.py:168
  333.7 3.2 collective-permute-start.53
  337.0 28.3 %collective-permute-start.55 = (f32[384,768]{1,0:T(8,128)S(1)}, f32[384,768]{1,0:T(8,128)S(1)}, u32[]{:S(2)}, u32[]{:S(2)}) collective-permute-start(f32[384,768]{1,0:T(8,128)S(1)} %slice_add_fusion.refs_12_), channel_id=1, source_target_pairs={{0,2},{1,3},{2,0},{3,1},{4,6},{5,7},{6,4},{7,5},{8,10},{9,11},{10,... | collective-permute-start | bytes 3538952 | tf_op jit(solution)/shard_map/ppermute | solution.py:168
  361.7 1.8 collective-permute-start.54
  361.9 2.2 collective-permute-start.57
  362.3 2.3 collective-permute-start.56
  (51 other events, 574.5 us)
Sparse Core Ops, SparseCore 0:
  72.2 37.3 all-gather.4
  250.3 35.3 all-gather.6

commit v2 on v1

--- a/solution.py
+++ b/solution.py
@@ -187,6 +187,28 @@
     return held[0]
 
 
+def join_kernel(n, *refs):
+    out_ref = refs[-1]
+    start = 0
+    for ref in refs[:n]:
+        out_ref[start : start + ref.shape[0], :] = ref[...]
+        start += ref.shape[0]
+
+
+def join(values, after):
+    rows = sum(value.shape[0] for value in values)
+    shape = jax.ShapeDtypeStruct((rows, values[0].shape[1]), values[0].dtype)
+    vmem = pl.BlockSpec(memory_space=pltpu.VMEM)
+    return pl.pallas_call(
+        functools.partial(join_kernel, len(values)),
+        in_specs=[vmem] * len(values) + [pl.BlockSpec(memory_space=pl.ANY)] * len(after),
+        out_specs=vmem,
+        out_shape=shape,
+        cost_estimate=pl.CostEstimate(flops=0, bytes_accessed=8 * shape.size, transcendentals=0),
+        name="join",
+    )(*values, *after)
+
+
 def line_hops(found, hops, n_row):
     for hop in hops:
         for way in (1, -1):
@@ -213,7 +235,9 @@
 
     found = [line_hops({0: chunk}, range(1, n_row), n_row) for chunk in chunks[:2]]
     shards = gather_relative(jnp.concatenate(chunks, axis=0), n_col)
-    picked, handed = pick([[f[d] for d in distances] for f in found], (place, away_at, n_col), chunks[2:])
+    begun = [found[-1][d] for d in (2, -2) if d in found[-1]]
+    handed = [join([chunk], begun) for chunk in chunks[2:]]
+    picked, _ = pick([[f[d] for d in distances] for f in found], (place, away_at, n_col))
 
     tiles = n_col * (shard // tile)
     pieces = []
@@ -226,12 +250,12 @@
 
     low = high = None
     for k in range(n):
-        if k >= 2:
-            line = lax.all_gather(handed[k - 2], "row")
-            (fetched,), _ = pick([[line]], (place, there_at, n_col), (), (low,) if k == 2 else (high,))
+        pieces.append([picked[k][0]] + [swap(picked[k][p], p, n_col) for p in range(1, n_col)])
+        high = apply(True, k, high, picked[k + 1][:1] if 0 < k < n - 1 else ())
+        if k + 2 < n:
+            line = lax.all_gather(handed[k], "row")
+            (fetched,), _ = pick([[line]], (place, there_at, n_col), (), (high,))
             picked.append(fetched)
-        pieces.append([picked[k][0]] + [swap(picked[k][p], p, n_col) for p in range(1, n_col)])
-        high = apply(True, k, high)
         if k < max(n - 2, 1):
             low = apply(False, k, low)
     far = scatter_relative([high[p * shard : (p + 1) * shard] for p in range(half)], n_col)

time: 378 us -> 450 us (1.19)
  waiting for transfers between devices: 86.6 us -> 130 us
  starting transfers between devices: 92.1 us -> 111 us
  Pallas kernels: 156 us -> 161 us
    ppermute x24, waiting for transfers between devices: 41.6 us -> 92.6 us  [line_hops(): found[way * hop] = lax.ppermute(found[way * (hop - 1)], 'row', pairs)]
    ppermute x24, starting transfers between devices: 70.5 us -> 88.7 us  [line_hops(): found[way * hop] = lax.ppermute(found[way * (hop - 1)], 'row', pairs)]
    ppermute x34, waiting for transfers between devices: 45 us -> 37.6 us  [swap(): return lax.ppermute(value, 'col', [(i, i ^ bit) for i in range(n_col)])]
    unnamed x111 -> x130, local copies, waits for them, and re-layouts: 18.8 us -> 22.8 us
  transfers between devices with their start and end apart: 60 -> 60, of which waited for: 36 -> 30; matrix products, arithmetic and copies ran while one was open for 1% -> 0% of each run, Pallas kernels for 35% -> 36%
where the time goes in v2:
time: 450 us; the launch traced here: 445 us
  Pallas kernels  161 us (36%)
  waiting for transfers between devices  130 us (29%)
  starting transfers between devices  111 us (25%)
  local copies, waits for them, and re-layouts  25.9 us (6%)
  between operations  14.5 us (3%)
    pallas_call x12, Pallas kernels, apply_chunk(): pl.pallas_call(functools.partial(apply_kernel, n, first, tiles), grid_spe...  144 us
    ppermute x24, waiting for transfers between devices, line_hops(): found[way * hop] = lax.ppermute(found[way * (hop - 1)], 'row', pairs)  92.6 us
    ppermute x24, starting transfers between devices, line_hops(): found[way * hop] = lax.ppermute(found[way * (hop - 1)], 'row', pairs)  88.7 us
    ppermute x34, waiting for transfers between devices, swap(): return lax.ppermute(value, 'col', [(i, i ^ bit) for i in range(n_col)])  37.6 us
    unnamed x130, local copies, waits for them, and re-layouts  22.8 us
    ppermute x34, starting transfers between devices, swap(): return lax.ppermute(value, 'col', [(i, i ^ bit) for i in range(n_col)])  21.8 us
    pallas_call x4, Pallas kernels, pick(): pl.pallas_call(functools.partial(pick_kernel, n_in, len(sets), first, n_o...  12.9 us
  transfers between devices with their start and end apart: 60, of which 30 were waited for; matrix products, arithmetic and copies ran while one was open for 0% of the time, Pallas kernels for 36%

profile of v2, /device:TPU:0, one launch (start us, length us, event | category | flops | bytes accessed | tf_op | source)
XLA Modules:
  0.0 444.9 jit_solution(12616638635225142149)
XLA Ops:
  6.5 2.2 fusion.8
  8.7 4.9 %collective-permute-start.1 = (f32[128,768]{1,0:T(8,128)S(1)}, f32[128,768]{1,0:T(8,128)S(1)}, u32[]{:S(2)}, u32[]{:S(2)}) collective-permute-start(f32[128,768]{1,0:T(8,128)S(1)} %get-tuple-element.66.refs_10_), channel_id=1, source_target_pairs={{0,4},{4,8},{8,12},{1,5},{5,9},{9,13},{2,6},{6,10},{10,14},{3,7},{... | collective-permute-start | bytes 1179656 | tf_op jit(solution)/shard_map/ppermute | solution.py:216
  13.7 1.3 collective-permute-start.3
  15.0 1.6 collective-permute-start.5
  16.5 5.5 %collective-permute-done.1.refs_11_ = f32[128,768]{1,0:T(8,128)S(1)} collective-permute-done((f32[128,768]{1,0:T(8,128)S(1)}, f32[128,768]{1,0:T(8,128)S(1)}, u32[]{:S(2)}, u32[]{:S(2)}) %collective-permute-start.1) | collective-permute-done | bytes 393248 | tf_op jit(solution)/shard_map/ppermute | solution.py:216
  22.0 4.4 collective-permute-start.2
  26.4 1.3 collective-permute-start.4
  27.7 6.1 %collective-permute-done.2.refs_1_.refs_12_ = f32[128,768]{1,0:T(8,128)S(1)} collective-permute-done((f32[128,768]{1,0:T(8,128)S(1)}, f32[128,768]{1,0:T(8,128)S(1)}, u32[]{:S(2)}, u32[]{:S(2)}) %collective-permute-start.2) | collective-permute-done | bytes 393248 | tf_op jit(solution)/shard_map/ppermute | solution.py:216
  33.9 4.3 collective-permute-done.4.refs_2_.refs_8_
  38.1 1.8 join.2
  41.3 4.6 %collective-permute-start.10 = (f32[128,768]{1,0:T(8,128)S(1)}, f32[128,768]{1,0:T(8,128)S(1)}, u32[]{:S(2)}, u32[]{:S(2)}) collective-permute-start(f32[128,768]{1,0:T(8,128)S(1)} %get-tuple-element.65.refs_3_), channel_id=1, source_target_pairs={{0,4},{4,8},{8,12},{1,5},{5,9},{9,13},{2,6},{6,10},{10,14},{3,7},{... | collective-permute-start | bytes 1179656 | tf_op jit(solution)/shard_map/ppermute | solution.py:216
  45.9 4.8 %collective-permute-done.7.refs_2_ = f32[128,768]{1,0:T(8,128)S(1)} collective-permute-done((f32[128,768]{1,0:T(8,128)S(1)}, f32[128,768]{1,0:T(8,128)S(1)}, u32[]{:S(2)}, u32[]{:S(2)}) %collective-permute-start.7) | collective-permute-done | bytes 393248 | tf_op jit(solution)/shard_map/ppermute | solution.py:216
  52.0 8.3 %collective-permute-done.10.refs_4_ = f32[128,768]{1,0:T(8,128)S(1)} collective-permute-done((f32[128,768]{1,0:T(8,128)S(1)}, f32[128,768]{1,0:T(8,128)S(1)}, u32[]{:S(2)}, u32[]{:S(2)}) %collective-permute-start.10) | collective-permute-done | bytes 393248 | tf_op jit(solution)/shard_map/ppermute | solution.py:216
  60.3 9.7 %collective-permute-start.11 = (f32[128,768]{1,0:T(8,128)S(1)}, f32[128,768]{1,0:T(8,128)}, u32[]{:S(2)}, u32[]{:S(2)}) collective-permute-start(f32[128,768]{1,0:T(8,128)S(1)} %collective-permute-done.10.refs_4_), channel_id=1, source_target_pairs={{0,4},{4,8},{8,12},{1,5},{5,9},{9,13},{2,6},{6,10},{10,14},{3,7},{... | collective-permute-start | bytes 1179656 | tf_op jit(solution)/shard_map/ppermute | solution.py:216
  70.1 11.2 %collective-permute-done.8.refs_1_ = f32[128,768]{1,0:T(8,128)} collective-permute-done((f32[128,768]{1,0:T(8,128)S(1)}, f32[128,768]{1,0:T(8,128)}, u32[]{:S(2)}, u32[]{:S(2)}) %collective-permute-start.8) | collective-permute-done | bytes 393248 | tf_op jit(solution)/shard_map/ppermute | solution.py:216
  83.0 9.1 %collective-permute-start.12 = (f32[128,768]{1,0:T(8,128)}, f32[128,768]{1,0:T(8,128)}, u32[]{:S(2)}, u32[]{:S(2)}) collective-permute-start(f32[128,768]{1,0:T(8,128)} %collective-permute-done.11.refs_5_), channel_id=1, source_target_pairs={{0,4},{4,8},{8,12},{1,5},{5,9},{9,13},{2,6},{6,10},{10,14},{3,7},{... | collective-permute-start | bytes 1179656 | tf_op jit(solution)/shard_map/ppermute | solution.py:216
  93.4 5.3 %collective-permute-start.14 = (f32[128,768]{1,0:T(8,128)}, f32[128,768]{1,0:T(8,128)}, u32[]{:S(2)}, u32[]{:S(2)}) collective-permute-start(f32[128,768]{1,0:T(8,128)} %copy-done.49), channel_id=1, source_target_pairs={{0,4},{4,8},{8,12},{1,5},{5,9},{9,13},{2,6},{6,10},{10,14},{3,7},{... | collective-permute-start | bytes 1179656 | tf_op jit(solution)/shard_map/ppermute | solution.py:216
  99.3 2.7 collective-permute-done.13.refs_7_
  102.0 1.5 collective-permute-done.14.refs_13_
  103.5 3.4 pick.4
  107.0 1.4 collective-permute-start.16
  110.2 9.0 %collective-permute-done.16.refs_5_ = f32[128,768]{1,0:T(8,128)S(1)} collective-permute-done((f32[128,768]{1,0:T(8,128)}, f32[128,768]{1,0:T(8,128)S(1)}, u32[]{:S(2)}, u32[]{:S(2)}) %collective-permute-start.16) | collective-permute-done | bytes 393248 | tf_op jit(solution)/shard_map/ppermute | solution.py:168
  119.2 1.4 collective-permute-start.22
  120.6 6.2 %collective-permute-done.17.refs_6_ = f32[128,768]{1,0:T(8,128)S(1)} collective-permute-done((f32[128,768]{1,0:T(8,128)}, f32[128,768]{1,0:T(8,128)S(1)}, u32[]{:S(2)}, u32[]{:S(2)}) %collective-permute-start.17) | collective-permute-done | bytes 393248 | tf_op jit(solution)/shard_map/ppermute | solution.py:168
  126.7 1.7 collective-permute-start.23
  129.7 11.7 %apply_chunk.12.refs_1_.refs_11_ = f32[768,768]{1,0:T(8,128)S(1)} custom-call(s32[24]{0:T(128)S(1)} %copy-done.37, f32[3,768]{1,0:T(4,128)S(1)} %broadcast_multiply_fusion.refs_0_, f32[384,768]{1,0:T(8,128)S(1)} %collective-permute-done.5.refs_1_, f32[384,768]{1,0:T(8,128)S(1)} %collective-permute-done.6.refs_2_, f32[128,768]{1,0:T(8,128)S(1)} %copy-done.21, ...), custom_call_target="tpu_custom_call" | custom-call | flops 7247757312 | bytes 11796480 | tf_op jit(solution)/shard_map/apply_chunk/pallas_call | solution.py:95
  141.5 1.4 copy-done
  145.1 3.0 pick.5
  154.7 12.1 %apply_chunk.14.refs_11_ = f32[768,768]{1,0:T(8,128)S(1)} custom-call(s32[24]{0:T(128)S(1)} %copy-done.38, f32[3,768]{1,0:T(4,128)S(1)} %broadcast_multiply_fusion.refs_0_, f32[384,768]{1,0:T(8,128)S(1)} %copy-done.6, f32[384,768]{1,0:T(8,128)S(1)} %copy-done.9, f32[128,768]{1,0:T(8,128)S(1)} %copy-done.17, ...), custom_call_target="tpu_custom_call", output_to_operand_aliasing={{}: (12, {})} | custom-call | flops 7247757312 | bytes 11796480 | tf_op jit(solution)/shard_map/apply_chunk/pallas_call | solution.py:95
  167.9 11.7 %apply_chunk.15 = f32[768,768]{1,0:T(8,128)S(1)} custom-call(s32[24]{0:T(128)S(1)} %copy-done.38, f32[3,768]{1,0:T(4,128)S(1)} %broadcast_multiply_fusion.refs_0_, f32[384,768]{1,0:T(8,128)S(1)} %copy-done.7, f32[384,768]{1,0:T(8,128)S(1)} %copy-done.9, f32[128,768]{1,0:T(8,128)S(1)} %copy-done.16, ...), custom_call_target="tpu_custom_call", output_to_operand_aliasing={{}: (12, {})} | custom-call | flops 7247757312 | bytes 11796480 | tf_op jit(solution)/shard_map/apply_chunk/pallas_call | solution.py:95
  181.0 12.3 %apply_chunk.13.refs_11_ = f32[768,768]{1,0:T(8,128)S(1)} custom-call(s32[24]{0:T(128)S(1)} %copy-done.38, f32[3,768]{1,0:T(4,128)S(1)} %broadcast_multiply_fusion.refs_0_, f32[384,768]{1,0:T(8,128)S(1)} %copy-done.4, f32[384,768]{1,0:T(8,128)} %collective-permute-done.refs_2_, f32[128,768]{1,0:T(8,128)S(1)} %copy-done.22, f32[128,768]{1,0:T(8,128)S(1)} %copy-done.26, ...), custom_call_target="tpu_custom_call" | custom-call | flops 7247757312 | bytes 11796480 | tf_op jit(solution)/shard_map/apply_chunk/pallas_call | solution.py:95
  194.4 12.4 %apply_chunk.16.refs_11_ = f32[768,768]{1,0:T(8,128)S(1)} custom-call(s32[24]{0:T(128)S(1)} %copy-done.38, f32[3,768]{1,0:T(4,128)S(1)} %broadcast_multiply_fusion.refs_0_, f32[384,768]{1,0:T(8,128)S(1)} %copy-done.4, f32[384,768]{1,0:T(8,128)} %collective-permute-done.refs_2_, f32[128,768]{1,0:T(8,128)S(1)} %copy-done.18, ...), custom_call_target="tpu_custom_call", output_to_operand_aliasing={{}: (12, {})} | custom-call | flops 7247757312 | bytes 11796480 | tf_op jit(solution)/shard_map/apply_chunk/pallas_call | solution.py:95
  206.8 12.1 %apply_chunk.17 = f32[768,768]{1,0:T(8,128)S(1)} custom-call(s32[24]{0:T(128)S(1)} %copy-done.38, f32[3,768]{1,0:T(4,128)S(1)} %broadcast_multiply_fusion.refs_0_, f32[384,768]{1,0:T(8,128)S(1)} %copy-done.4, f32[384,768]{1,0:T(8,128)} %collective-permute-done.refs_2_, f32[128,768]{1,0:T(8,128)S(1)} %copy-done.16, ...), custom_call_target="tpu_custom_call", output_to_operand_aliasing={{}: (12, {})} | custom-call | flops 7247757312 | bytes 11796480 | tf_op jit(solution)/shard_map/apply_chunk/pallas_call | solution.py:95
  222.2 4.6 %collective-permute-start.30 = (f32[128,768]{1,0:T(8,128)S(1)}, f32[128,768]{1,0:T(8,128)S(1)}, u32[]{:S(2)}, u32[]{:S(2)}) collective-permute-start(f32[128,768]{1,0:T(8,128)S(1)} %get-tuple-element.55.refs_10_), channel_id=1, source_target_pairs={{0,4},{4,8},{8,12},{1,5},{5,9},{9,13},{2,6},{6,10},{10,14},{3,7},{... | collective-permute-start | bytes 1179656 | tf_op jit(solution)/shard_map/ppermute | solution.py:216
  228.2 1.3 collective-permute-start.34
  229.6 5.8 %collective-permute-done.30.refs_11_ = f32[128,768]{1,0:T(8,128)S(1)} collective-permute-done((f32[128,768]{1,0:T(8,128)S(1)}, f32[128,768]{1,0:T(8,128)S(1)}, u32[]{:S(2)}, u32[]{:S(2)}) %collective-permute-start.30) | collective-permute-done | bytes 393248 | tf_op jit(solution)/shard_map/ppermute | solution.py:216
  235.4 4.4 collective-permute-start.31
  239.9 1.3 collective-permute-start.33
  241.2 6.6 %collective-permute-done.31.refs_1_.refs_12_ = f32[128,768]{1,0:T(8,128)S(1)} collective-permute-done((f32[128,768]{1,0:T(8,128)S(1)}, f32[128,768]{1,0:T(8,128)S(1)}, u32[]{:S(2)}, u32[]{:S(2)}) %collective-permute-start.31) | collective-permute-done | bytes 393248 | tf_op jit(solution)/shard_map/ppermute | solution.py:216
  247.8 4.4 collective-permute-done.33.refs_2_.refs_8_
  253.0 1.8 join.3
  256.1 4.6 %collective-permute-start.39 = (f32[128,768]{1,0:T(8,128)S(1)}, f32[128,768]{1,0:T(8,128)S(1)}, u32[]{:S(2)}, u32[]{:S(2)}) collective-permute-start(f32[128,768]{1,0:T(8,128)S(1)} %get-tuple-element.53.refs_3_), channel_id=1, source_target_pairs={{0,4},{4,8},{8,12},{1,5},{5,9},{9,13},{2,6},{6,10},{10,14},{3,7},{... | collective-permute-start | bytes 1179656 | tf_op jit(solution)/shard_map/ppermute | solution.py:216
  260.7 7.4 %collective-permute-done.36.refs_2_ = f32[128,768]{1,0:T(8,128)S(1)} collective-permute-done((f32[128,768]{1,0:T(8,128)S(1)}, f32[128,768]{1,0:T(8,128)S(1)}, u32[]{:S(2)}, u32[]{:S(2)}) %collective-permute-start.36) | collective-permute-done | bytes 393248 | tf_op jit(solution)/shard_map/ppermute | solution.py:216
  269.4 6.0 %collective-permute-done.39.refs_4_ = f32[128,768]{1,0:T(8,128)S(1)} collective-permute-done((f32[128,768]{1,0:T(8,128)S(1)}, f32[128,768]{1,0:T(8,128)S(1)}, u32[]{:S(2)}, u32[]{:S(2)}) %collective-permute-start.39) | collective-permute-done | bytes 393248 | tf_op jit(solution)/shard_map/ppermute | solution.py:216
  275.4 9.3 %collective-permute-start.40 = (f32[128,768]{1,0:T(8,128)S(1)}, f32[128,768]{1,0:T(8,128)S(1)}, u32[]{:S(2)}, u32[]{:S(2)}) collective-permute-start(f32[128,768]{1,0:T(8,128)S(1)} %collective-permute-done.39.refs_4_), channel_id=1, source_target_pairs={{0,4},{4,8},{8,12},{1,5},{5,9},{9,13},{2,6},{6,10},{10,14},{3,7},{... | collective-permute-start | bytes 1179656 | tf_op jit(solution)/shard_map/ppermute | solution.py:216
  284.8 13.0 %collective-permute-done.37.refs_1_ = f32[128,768]{1,0:T(8,128)S(1)} collective-permute-done((f32[128,768]{1,0:T(8,128)S(1)}, f32[128,768]{1,0:T(8,128)S(1)}, u32[]{:S(2)}, u32[]{:S(2)}) %collective-permute-start.37) | collective-permute-done | bytes 393248 | tf_op jit(solution)/shard_map/ppermute | solution.py:216
  299.1 6.5 %collective-permute-start.41 = (f32[128,768]{1,0:T(8,128)S(1)}, f32[128,768]{1,0:T(8,128)S(1)}, u32[]{:S(2)}, u32[]{:S(2)}) collective-permute-start(f32[128,768]{1,0:T(8,128)S(1)} %collective-permute-done.40.refs_5_), channel_id=1, source_target_pairs={{0,4},{4,8},{8,12},{1,5},{5,9},{9,13},{2,6},{6,10},{10,14},{3,7},{... | collective-permute-start | bytes 1179656 | tf_op jit(solution)/shard_map/ppermute | solution.py:216
  307.0 5.8 %collective-permute-start.43 = (f32[128,768]{1,0:T(8,128)}, f32[128,768]{1,0:T(8,128)}, u32[]{:S(2)}, u32[]{:S(2)}) collective-permute-start(f32[128,768]{1,0:T(8,128)} %copy-done.50), channel_id=1, source_target_pairs={{0,4},{4,8},{8,12},{1,5},{5,9},{9,13},{2,6},{6,10},{10,14},{3,7},{... | collective-permute-start | bytes 1179656 | tf_op jit(solution)/shard_map/ppermute | solution.py:216
  313.8 3.0 collective-permute-done.42.refs_7_
  318.1 3.5 pick.6
  321.7 1.6 collective-permute-start.45
  324.1 9.8 %collective-permute-done.45.refs_5_ = f32[128,768]{1,0:T(8,128)S(1)} collective-permute-done((f32[128,768]{1,0:T(8,128)}, f32[128,768]{1,0:T(8,128)S(1)}, u32[]{:S(2)}, u32[]{:S(2)}) %collective-permute-start.45) | collective-permute-done | bytes 393248 | tf_op jit(solution)/shard_map/ppermute | solution.py:168
  333.9 1.6 collective-permute-start.51
  335.4 6.0 %collective-permute-done.46.refs_6_ = f32[128,768]{1,0:T(8,128)S(1)} collective-permute-done((f32[128,768]{1,0:T(8,128)}, f32[128,768]{1,0:T(8,128)S(1)}, u32[]{:S(2)}, u32[]{:S(2)}) %collective-permute-start.46) | collective-permute-done | bytes 393248 | tf_op jit(solution)/shard_map/ppermute | solution.py:168
  341.5 1.8 collective-permute-start.52
  344.6 11.6 %apply_chunk.18.refs_1_.refs_11_ = f32[768,768]{1,0:T(8,128)S(1)} custom-call(s32[24]{0:T(128)S(1)} %copy-done.39, f32[3,768]{1,0:T(4,128)S(1)} %broadcast_multiply_fusion.refs_0_, f32[384,768]{1,0:T(8,128)S(1)} %collective-permute-done.34.refs_1_, f32[384,768]{1,0:T(8,128)S(1)} %collective-permute-done.35.refs_2_, f32[128,768]{1,0:T(8,128)S(1)} %copy-done.23, ...), custom_call_target="tpu_custom_call" | custom-call | flops 7247757312 | bytes 11796480 | tf_op jit(solution)/shard_map/apply_chunk/pallas_call | solution.py:95
  356.2 1.4 copy-done.2
  359.8 3.0 pick.7
  363.4 1.3 collective-permute-start.49
  369.3 12.1 %apply_chunk.20.refs_11_ = f32[768,768]{1,0:T(8,128)S(1)} custom-call(s32[24]{0:T(128)S(1)} %copy-done.40, f32[3,768]{1,0:T(4,128)S(1)} %broadcast_multiply_fusion.refs_0_, f32[384,768]{1,0:T(8,128)S(1)} %copy-done.11, f32[384,768]{1,0:T(8,128)S(1)} %copy-done.14, f32[128,768]{1,0:T(8,128)S(1)} %copy-done.19, ...), custom_call_target="tpu_custom_call", output_to_operand_aliasing={{}: (12, {})} | custom-call | flops 7247757312 | bytes 11796480 | tf_op jit(solution)/shard_map/apply_chunk/pallas_call | solution.py:95
  382.6 11.7 %apply_chunk.21 = f32[768,768]{1,0:T(8,128)S(1)} custom-call(s32[24]{0:T(128)S(1)} %copy-done.40, f32[3,768]{1,0:T(4,128)S(1)} %broadcast_multiply_fusion.refs_0_, f32[384,768]{1,0:T(8,128)S(1)} %copy-done.12, f32[384,768]{1,0:T(8,128)S(1)} %copy-done.14, f32[128,768]{1,0:T(8,128)S(1)} %copy-done.15, ...), custom_call_target="tpu_custom_call", output_to_operand_aliasing={{}: (12, {})} | custom-call | flops 7247757312 | bytes 11796480 | tf_op jit(solution)/shard_map/apply_chunk/pallas_call | solution.py:95
  395.7 12.1 %apply_chunk.19.refs_11_ = f32[768,768]{1,0:T(8,128)S(1)} custom-call(s32[24]{0:T(128)S(1)} %copy-done.40, f32[3,768]{1,0:T(4,128)S(1)} %broadcast_multiply_fusion.refs_0_, f32[384,768]{1,0:T(8,128)S(1)} %pad_maximum_fusion.refs_1_, f32[384,768]{1,0:T(8,128)} %collective-permute-done.29.refs_2_, f32[128,768]{1,0:T(8,128)S(1)} %copy-done.24, ...), custom_call_target="tpu_custom_call" | custom-call | flops 7247757312 | bytes 11796480 | tf_op jit(solution)/shard_map/apply_chunk/pallas_call | solution.py:95
  408.8 12.4 %apply_chunk.22.refs_11_ = f32[768,768]{1,0:T(8,128)S(1)} custom-call(s32[24]{0:T(128)S(1)} %copy-done.40, f32[3,768]{1,0:T(4,128)S(1)} %broadcast_multiply_fusion.refs_0_, f32[384,768]{1,0:T(8,128)S(1)} %pad_maximum_fusion.refs_1_, f32[384,768]{1,0:T(8,128)} %collective-permute-done.29.refs_2_, ...), custom_call_target="tpu_custom_call", output_to_operand_aliasing={{}: (12, {})} | custom-call | flops 7247757312 | bytes 11796480 | tf_op jit(solution)/shard_map/apply_chunk/pallas_call | solution.py:95
  421.3 12.1 %apply_chunk.23 = f32[768,768]{1,0:T(8,128)S(1)} custom-call(s32[24]{0:T(128)S(1)} %copy-done.40, f32[3,768]{1,0:T(4,128)S(1)} %broadcast_multiply_fusion.refs_0_, f32[384,768]{1,0:T(8,128)S(1)} %pad_maximum_fusion.refs_1_, f32[384,768]{1,0:T(8,128)} %collective-permute-done.29.refs_2_, f32[128,768]{1,0:T(8,128)S(1)} %copy-done.15, ...), custom_call_target="tpu_custom_call", output_to_operand_aliasing={{}: (12, {})} | custom-call | flops 7247757312 | bytes 11796480 | tf_op jit(solution)/shard_map/apply_chunk/pallas_call | solution.py:95
  (219 shorter events, 52.2 us)
Async XLA Ops:
  6.5 138.6 %all-gather.5.cloned.1.call-start = ((), (), s32[]{:S(2)}) async-start(), calls=%async_computation | async-start | bytes 1966080 | tf_op jit(solution)/shard_map/all_gather | solution.py:256
  8.7 61.3 %copy-start.47 = (f32[128,768]{1,0:T(8,128)}, f32[128,768]{1,0:T(8,128)S(1)}, u32[]{:S(2)}) copy-start(f32[128,768]{1,0:T(8,128)S(1)} %get-tuple-element.65.refs_3_) | copy-start | bytes 1179652
  8.7 61.3 %copy-start.48 = (f32[128,768]{1,0:T(8,128)}, f32[128,768]{1,0:T(8,128)S(1)}, u32[]{:S(2)}) copy-start(f32[128,768]{1,0:T(8,128)S(1)} %get-tuple-element.66.refs_10_) | copy-start | bytes 1179652
  8.7 13.3 %collective-permute-start.1 = (f32[128,768]{1,0:T(8,128)S(1)}, f32[128,768]{1,0:T(8,128)S(1)}, u32[]{:S(2)}, u32[]{:S(2)}) collective-permute-start(f32[128,768]{1,0:T(8,128)S(1)} %get-tuple-element.66.refs_10_), channel_id=1, source_target_pairs={{0,4},{4,8},{8,12},{1,5},{5,9},{9,13},{2,6},{6,10},{10,14},{3,7},{... | collective-permute-start | bytes 1179656 | tf_op jit(solution)/shard_map/ppermute | solution.py:216
  13.7 12.7 %collective-permute-start.3 = (f32[128,768]{1,0:T(8,128)S(1)}, f32[128,768]{1,0:T(8,128)S(1)}, u32[]{:S(2)}, u32[]{:S(2)}) collective-permute-start(f32[128,768]{1,0:T(8,128)S(1)} %get-tuple-element.66.refs_10_), channel_id=1, source_target_pairs={{4,0},{8,4},{12,8},{5,1},{9,5},{13,9},{6,2},{10,6},{14,10},{7,3},{... | collective-permute-start | bytes 1179656 | tf_op jit(solution)/shard_map/ppermute | solution.py:216
  15.0 55.1 %collective-permute-start.5 = (f32[384,768]{1,0:T(8,128)S(1)}, f32[384,768]{1,0:T(8,128)S(1)}, u32[]{:S(2)}, u32[]{:S(2)}) collective-permute-start(f32[384,768]{1,0:T(8,128)S(1)} %copy-done.4), channel_id=1, source_target_pairs={{0,2},{1,3},{2,0},{3,1},{4,6},{5,7},{6,4},{7,5},{8,10},{9,11},{10,... | collective-permute-start | bytes 3538952 | tf_op jit(solution)/shard_map/ppermute | solution.py:168
  22.0 11.9 %collective-permute-start.2 = (f32[128,768]{1,0:T(8,128)S(1)}, f32[128,768]{1,0:T(8,128)S(1)}, u32[]{:S(2)}, u32[]{:S(2)}) collective-permute-start(f32[128,768]{1,0:T(8,128)S(1)} %collective-permute-done.1.refs_11_), channel_id=1, source_target_pairs={{0,4},{4,8},{8,12},{1,5},{5,9},{9,13},{2,6},{6,10},{10,14},{3,7},{... | collective-permute-start | bytes 1179656 | tf_op jit(solution)/shard_map/ppermute | solution.py:216
  26.4 11.7 %collective-permute-start.4 = (f32[128,768]{1,0:T(8,128)S(1)}, f32[128,768]{1,0:T(8,128)}, u32[]{:S(2)}, u32[]{:S(2)}) collective-permute-start(f32[128,768]{1,0:T(8,128)S(1)} %collective-permute-done.3.refs_9_), channel_id=1, source_target_pairs={{4,0},{8,4},{12,8},{5,1},{9,5},{13,9},{6,2},{10,6},{14,10},{7,3},{... | collective-permute-start | bytes 1179656 | tf_op jit(solution)/shard_map/ppermute | solution.py:216
  40.0 319.9 %all-gather.7.cloned.1.call-start = ((), (), s32[]{:S(2)}) async-start(), calls=%async_computation.1 | async-start | bytes 1966080 | tf_op jit(solution)/shard_map/all_gather | solution.py:256
  40.0 10.7 %collective-permute-start.7 = (f32[128,768]{1,0:T(8,128)S(1)}, f32[128,768]{1,0:T(8,128)S(1)}, u32[]{:S(2)}, u32[]{:S(2)}) collective-permute-start(f32[128,768]{1,0:T(8,128)S(1)} %get-tuple-element.65.refs_3_), channel_id=1, source_target_pairs={{4,0},{8,4},{12,8},{5,1},{9,5},{13,9},{6,2},{10,6},{14,10},{7,3},{... | collective-permute-start | bytes 1179656 | tf_op jit(solution)/shard_map/ppermute | solution.py:216
  41.3 19.0 %collective-permute-start.10 = (f32[128,768]{1,0:T(8,128)S(1)}, f32[128,768]{1,0:T(8,128)S(1)}, u32[]{:S(2)}, u32[]{:S(2)}) collective-permute-start(f32[128,768]{1,0:T(8,128)S(1)} %get-tuple-element.65.refs_3_), channel_id=1, source_target_pairs={{0,4},{4,8},{8,12},{1,5},{5,9},{9,13},{2,6},{6,10},{10,14},{3,7},{... | collective-permute-start | bytes 1179656 | tf_op jit(solution)/shard_map/ppermute | solution.py:216
  50.7 30.7 %collective-permute-start.8 = (f32[128,768]{1,0:T(8,128)S(1)}, f32[128,768]{1,0:T(8,128)}, u32[]{:S(2)}, u32[]{:S(2)}) collective-permute-start(f32[128,768]{1,0:T(8,128)S(1)} %collective-permute-done.7.refs_2_), channel_id=1, source_target_pairs={{4,0},{8,4},{12,8},{5,1},{9,5},{13,9},{6,2},{10,6},{14,10},{7,3},{... | collective-permute-start | bytes 1179656 | tf_op jit(solution)/shard_map/ppermute | solution.py:216
  60.3 22.6 %collective-permute-start.11 = (f32[128,768]{1,0:T(8,128)S(1)}, f32[128,768]{1,0:T(8,128)}, u32[]{:S(2)}, u32[]{:S(2)}) collective-permute-start(f32[128,768]{1,0:T(8,128)S(1)} %collective-permute-done.10.refs_4_), channel_id=1, source_target_pairs={{0,4},{4,8},{8,12},{1,5},{5,9},{9,13},{2,6},{6,10},{10,14},{3,7},{... | collective-permute-start | bytes 1179656 | tf_op jit(solution)/shard_map/ppermute | solution.py:216
  70.1 58.4 %collective-permute-start.6 = (f32[384,768]{1,0:T(8,128)S(1)}, f32[384,768]{1,0:T(8,128)S(1)}, u32[]{:S(2)}, u32[]{:S(2)}) collective-permute-start(f32[384,768]{1,0:T(8,128)S(1)} %collective-permute-done.5.refs_1_), channel_id=1, source_target_pairs={{0,1},{1,0},{2,3},{3,2},{4,5},{5,4},{6,7},{7,6},{8,9},{9,8},{10,11... | collective-permute-start | bytes 3538952 | tf_op jit(solution)/shard_map/ppermute | solution.py:168
  81.4 18.0 %collective-permute-start.9 = (f32[128,768]{1,0:T(8,128)}, f32[128,768]{1,0:T(8,128)}, u32[]{:S(2)}, u32[]{:S(2)}) collective-permute-start(f32[128,768]{1,0:T(8,128)} %collective-permute-done.8.refs_1_), channel_id=1, source_target_pairs={{4,0},{8,4},{12,8},{5,1},{9,5},{13,9},{6,2},{10,6},{14,10},{7,3},{... | collective-permute-start | bytes 1179656 | tf_op jit(solution)/shard_map/ppermute | solution.py:216
  83.0 16.4 %collective-permute-start.12 = (f32[128,768]{1,0:T(8,128)}, f32[128,768]{1,0:T(8,128)}, u32[]{:S(2)}, u32[]{:S(2)}) collective-permute-start(f32[128,768]{1,0:T(8,128)} %collective-permute-done.11.refs_5_), channel_id=1, source_target_pairs={{0,4},{4,8},{8,12},{1,5},{5,9},{9,13},{2,6},{6,10},{10,14},{3,7},{... | collective-permute-start | bytes 1179656 | tf_op jit(solution)/shard_map/ppermute | solution.py:216
  92.1 10.0 %collective-permute-start.13 = (f32[128,768]{1,0:T(8,128)}, f32[128,768]{1,0:T(8,128)}, u32[]{:S(2)}, u32[]{:S(2)}) collective-permute-start(f32[128,768]{1,0:T(8,128)} %collective-permute-done.4.refs_2_.refs_8_), channel_id=1, source_target_pairs={{4,0},{8,4},{12,8},{5,1},{9,5},{13,9},{6,2},{10,6},{14,10},{7,3},{... | collective-permute-start | bytes 1179656 | tf_op jit(solution)/shard_map/ppermute | solution.py:216
  93.4 10.1 %collective-permute-start.14 = (f32[128,768]{1,0:T(8,128)}, f32[128,768]{1,0:T(8,128)}, u32[]{:S(2)}, u32[]{:S(2)}) collective-permute-start(f32[128,768]{1,0:T(8,128)} %copy-done.49), channel_id=1, source_target_pairs={{0,4},{4,8},{8,12},{1,5},{5,9},{9,13},{2,6},{6,10},{10,14},{3,7},{... | collective-permute-start | bytes 1179656 | tf_op jit(solution)/shard_map/ppermute | solution.py:216
  106.9 3.1 collective-permute-start.15
  107.0 12.2 %collective-permute-start.16 = (f32[128,768]{1,0:T(8,128)}, f32[128,768]{1,0:T(8,128)S(1)}, u32[]{:S(2)}, u32[]{:S(2)}) collective-permute-start(f32[128,768]{1,0:T(8,128)} %get-tuple-element.31), channel_id=1, source_target_pairs={{0,2},{1,3},{2,0},{3,1},{4,6},{5,7},{6,4},{7,5},{8,10},{9,11},{10,... | collective-permute-start | bytes 1179656 | tf_op jit(solution)/shard_map/ppermute | solution.py:168
  108.5 18.3 %collective-permute-start.17 = (f32[128,768]{1,0:T(8,128)}, f32[128,768]{1,0:T(8,128)S(1)}, u32[]{:S(2)}, u32[]{:S(2)}) collective-permute-start(f32[128,768]{1,0:T(8,128)} %get-tuple-element.32), channel_id=1, source_target_pairs={{0,3},{1,2},{2,1},{3,0},{4,7},{5,6},{6,5},{7,4},{8,11},{9,10},{10,... | collective-permute-start | bytes 1179656 | tf_op jit(solution)/shard_map/ppermute | solution.py:168
  108.9 71.3 %collective-permute-start = (f32[384,768]{1,0:T(8,128)S(1)}, f32[384,768]{1,0:T(8,128)}, u32[]{:S(2)}, u32[]{:S(2)}) collective-permute-start(f32[384,768]{1,0:T(8,128)S(1)} %copy-done.4), channel_id=1, source_target_pairs={{0,1},{1,0},{2,3},{3,2},{4,5},{5,4},{6,7},{7,6},{8,9},{9,8},{10,11... | collective-permute-start | bytes 3538952 | tf_op jit(solution)/shard_map/ppermute | solution.py:168
  110.0 38.2 %collective-permute-start.21 = (f32[128,768]{1,0:T(8,128)}, f32[128,768]{1,0:T(8,128)}, u32[]{:S(2)}, u32[]{:S(2)}) collective-permute-start(f32[128,768]{1,0:T(8,128)} %get-tuple-element.38), channel_id=1, source_target_pairs={{0,1},{1,0},{2,3},{3,2},{4,5},{5,4},{6,7},{7,6},{8,9},{9,8},{10,11... | collective-permute-start | bytes 1179656 | tf_op jit(solution)/shard_map/ppermute | solution.py:168
  119.2 29.8 %collective-permute-start.22 = (f32[128,768]{1,0:T(8,128)}, f32[128,768]{1,0:T(8,128)}, u32[]{:S(2)}, u32[]{:S(2)}) collective-permute-start(f32[128,768]{1,0:T(8,128)} %get-tuple-element.39), channel_id=1, source_target_pairs={{0,2},{1,3},{2,0},{3,1},{4,6},{5,7},{6,4},{7,5},{8,10},{9,11},{10,... | collective-permute-start | bytes 1179656 | tf_op jit(solution)/shard_map/ppermute | solution.py:168
  126.7 23.4 %collective-permute-start.23 = (f32[128,768]{1,0:T(8,128)}, f32[128,768]{1,0:T(8,128)}, u32[]{:S(2)}, u32[]{:S(2)}) collective-permute-start(f32[128,768]{1,0:T(8,128)} %get-tuple-element.40), channel_id=1, source_target_pairs={{0,3},{1,2},{2,1},{3,0},{4,7},{5,6},{6,5},{7,4},{8,11},{9,10},{10,... | collective-permute-start | bytes 1179656 | tf_op jit(solution)/shard_map/ppermute | solution.py:168
  148.2 18.6 %collective-permute-start.18 = (f32[128,768]{1,0:T(8,128)}, f32[128,768]{1,0:T(8,128)S(1)}, u32[]{:S(2)}, u32[]{:S(2)}) collective-permute-start(f32[128,768]{1,0:T(8,128)} %get-tuple-element.34), channel_id=1, source_target_pairs={{0,1},{1,0},{2,3},{3,2},{4,5},{5,4},{6,7},{7,6},{8,9},{9,8},{10,11... | collective-permute-start | bytes 1179656 | tf_op jit(solution)/shard_map/ppermute | solution.py:168
  148.2 18.5 %collective-permute-start.19 = (f32[128,768]{1,0:T(8,128)}, f32[128,768]{1,0:T(8,128)S(1)}, u32[]{:S(2)}, u32[]{:S(2)}) collective-permute-start(f32[128,768]{1,0:T(8,128)} %get-tuple-element.35), channel_id=1, source_target_pairs={{0,2},{1,3},{2,0},{3,1},{4,6},{5,7},{6,4},{7,5},{8,10},{9,11},{10,... | collective-permute-start | bytes 1179656 | tf_op jit(solution)/shard_map/ppermute | solution.py:168
  149.0 19.0 %collective-permute-start.20 = (f32[128,768]{1,0:T(8,128)}, f32[128,768]{1,0:T(8,128)S(1)}, u32[]{:S(2)}, u32[]{:S(2)}) collective-permute-start(f32[128,768]{1,0:T(8,128)} %get-tuple-element.36), channel_id=1, source_target_pairs={{0,3},{1,2},{2,1},{3,0},{4,7},{5,6},{6,5},{7,4},{8,11},{9,10},{10,... | collective-permute-start | bytes 1179656 | tf_op jit(solution)/shard_map/ppermute | solution.py:168
  179.8 13.6 %collective-permute-start.24 = (f32[384,768]{1,0:T(8,128)S(1)}, f32[384,768]{1,0:T(8,128)S(1)}, u32[]{:S(2)}, u32[]{:S(2)}) collective-permute-start(f32[384,768]{1,0:T(8,128)S(1)} %slice.102), channel_id=1, source_target_pairs={{0,1},{1,0},{2,3},{3,2},{4,5},{5,4},{6,7},{7,6},{8,9},{9,8},{10,11... | collective-permute-start | bytes 3538952 | tf_op jit(solution)/shard_map/ppermute | solution.py:168
  193.5 28.3 %collective-permute-start.26 = (f32[384,768]{1,0:T(8,128)S(1)}, f32[384,768]{1,0:T(8,128)S(1)}, u32[]{:S(2)}, u32[]{:S(2)}) collective-permute-start(f32[384,768]{1,0:T(8,128)S(1)} %slice_add_fusion.1.refs_12_), channel_id=1, source_target_pairs={{0,2},{1,3},{2,0},{3,1},{4,6},{5,7},{6,4},{7,5},{8,10},{9,11},{10,... | collective-permute-start | bytes 3538952 | tf_op jit(solution)/shard_map/ppermute | solution.py:168
  219.0 1.8 collective-permute-start.25
  219.3 2.0 collective-permute-start.28
  219.5 2.3 collective-permute-start.27
  222.2 13.2 %collective-permute-start.30 = (f32[128,768]{1,0:T(8,128)S(1)}, f32[128,768]{1,0:T(8,128)S(1)}, u32[]{:S(2)}, u32[]{:S(2)}) collective-permute-start(f32[128,768]{1,0:T(8,128)S(1)} %get-tuple-element.55.refs_10_), channel_id=1, source_target_pairs={{0,4},{4,8},{8,12},{1,5},{5,9},{9,13},{2,6},{6,10},{10,14},{3,7},{... | collective-permute-start | bytes 1179656 | tf_op jit(solution)/shard_map/ppermute | solution.py:216
  226.8 13.0 %collective-permute-start.32 = (f32[128,768]{1,0:T(8,128)S(1)}, f32[128,768]{1,0:T(8,128)S(1)}, u32[]{:S(2)}, u32[]{:S(2)}) collective-permute-start(f32[128,768]{1,0:T(8,128)S(1)} %get-tuple-element.55.refs_10_), channel_id=1, source_target_pairs={{4,0},{8,4},{12,8},{5,1},{9,5},{13,9},{6,2},{10,6},{14,10},{7,3},{... | collective-permute-start | bytes 1179656 | tf_op jit(solution)/shard_map/ppermute | solution.py:216
  228.2 56.5 %collective-permute-start.34 = (f32[384,768]{1,0:T(8,128)S(1)}, f32[384,768]{1,0:T(8,128)S(1)}, u32[]{:S(2)}, u32[]{:S(2)}) collective-permute-start(f32[384,768]{1,0:T(8,128)S(1)} %pad_maximum_fusion.refs_1_), channel_id=1, source_target_pairs={{0,2},{1,3},{2,0},{3,1},{4,6},{5,7},{6,4},{7,5},{8,10},{9,11},{10,... | collective-permute-start | bytes 3538952 | tf_op jit(solution)/shard_map/ppermute | solution.py:168
  235.4 12.4 %collective-permute-start.31 = (f32[128,768]{1,0:T(8,128)S(1)}, f32[128,768]{1,0:T(8,128)S(1)}, u32[]{:S(2)}, u32[]{:S(2)}) collective-permute-start(f32[128,768]{1,0:T(8,128)S(1)} %collective-permute-done.30.refs_11_), channel_id=1, source_target_pairs={{0,4},{4,8},{8,12},{1,5},{5,9},{9,13},{2,6},{6,10},{10,14},{3,7},{... | collective-permute-start | bytes 1179656 | tf_op jit(solution)/shard_map/ppermute | solution.py:216
  239.9 12.4 %collective-permute-start.33 = (f32[128,768]{1,0:T(8,128)S(1)}, f32[128,768]{1,0:T(8,128)S(1)}, u32[]{:S(2)}, u32[]{:S(2)}) collective-permute-start(f32[128,768]{1,0:T(8,128)S(1)} %collective-permute-done.32.refs_9_), channel_id=1, source_target_pairs={{4,0},{8,4},{12,8},{5,1},{9,5},{13,9},{6,2},{10,6},{14,10},{7,3},{... | collective-permute-start | bytes 1179656 | tf_op jit(solution)/shard_map/ppermute | solution.py:216
  254.8 88.5 %copy-start.39 = (s32[24]{0:T(128)S(1)}, s32[24]{0:T(128)}, u32[]{:S(2)}) copy-start(s32[24]{0:T(128)} %stack.112.which.place) | copy-start | bytes 292
  254.8 13.3 %collective-permute-start.36 = (f32[128,768]{1,0:T(8,128)S(1)}, f32[128,768]{1,0:T(8,128)S(1)}, u32[]{:S(2)}, u32[]{:S(2)}) collective-permute-start(f32[128,768]{1,0:T(8,128)S(1)} %get-tuple-element.53.refs_3_), channel_id=1, source_target_pairs={{4,0},{8,4},{12,8},{5,1},{9,5},{13,9},{6,2},{10,6},{14,10},{7,3},{... | collective-permute-start | bytes 1179656 | tf_op jit(solution)/shard_map/ppermute | solution.py:216
  256.1 19.3 %collective-permute-start.39 = (f32[128,768]{1,0:T(8,128)S(1)}, f32[128,768]{1,0:T(8,128)S(1)}, u32[]{:S(2)}, u32[]{:S(2)}) collective-permute-start(f32[128,768]{1,0:T(8,128)S(1)} %get-tuple-element.53.refs_3_), channel_id=1, source_target_pairs={{0,4},{4,8},{8,12},{1,5},{5,9},{9,13},{2,6},{6,10},{10,14},{3,7},{... | collective-permute-start | bytes 1179656 | tf_op jit(solution)/shard_map/ppermute | solution.py:216
  268.1 29.7 %collective-permute-start.37 = (f32[128,768]{1,0:T(8,128)S(1)}, f32[128,768]{1,0:T(8,128)S(1)}, u32[]{:S(2)}, u32[]{:S(2)}) collective-permute-start(f32[128,768]{1,0:T(8,128)S(1)} %collective-permute-done.36.refs_2_), channel_id=1, source_target_pairs={{4,0},{8,4},{12,8},{5,1},{9,5},{13,9},{6,2},{10,6},{14,10},{7,3},{... | collective-permute-start | bytes 1179656 | tf_op jit(solution)/shard_map/ppermute | solution.py:216
  275.4 23.7 %collective-permute-start.40 = (f32[128,768]{1,0:T(8,128)S(1)}, f32[128,768]{1,0:T(8,128)S(1)}, u32[]{:S(2)}, u32[]{:S(2)}) collective-permute-start(f32[128,768]{1,0:T(8,128)S(1)} %collective-permute-done.39.refs_4_), channel_id=1, source_target_pairs={{0,4},{4,8},{8,12},{1,5},{5,9},{9,13},{2,6},{6,10},{10,14},{3,7},{... | collective-permute-start | bytes 1179656 | tf_op jit(solution)/shard_map/ppermute | solution.py:216
  284.7 58.6 %copy-start.10 = (f32[384,768]{1,0:T(8,128)}, f32[384,768]{1,0:T(8,128)S(1)}, u32[]{:S(2)}) copy-start(f32[384,768]{1,0:T(8,128)S(1)} %collective-permute-done.34.refs_1_) | copy-start | bytes 3538948
  284.7 58.5 %collective-permute-start.35 = (f32[384,768]{1,0:T(8,128)S(1)}, f32[384,768]{1,0:T(8,128)S(1)}, u32[]{:S(2)}, u32[]{:S(2)}) collective-permute-start(f32[384,768]{1,0:T(8,128)S(1)} %collective-permute-done.34.refs_1_), channel_id=1, source_target_pairs={{0,1},{1,0},{2,3},{3,2},{4,5},{5,4},{6,7},{7,6},{8,9},{9,8},{10,11... | collective-permute-start | bytes 3538952 | tf_op jit(solution)/shard_map/ppermute | solution.py:168
  297.8 14.9 %collective-permute-start.38 = (f32[128,768]{1,0:T(8,128)S(1)}, f32[128,768]{1,0:T(8,128)S(1)}, u32[]{:S(2)}, u32[]{:S(2)}) collective-permute-start(f32[128,768]{1,0:T(8,128)S(1)} %collective-permute-done.37.refs_1_), channel_id=1, source_target_pairs={{4,0},{8,4},{12,8},{5,1},{9,5},{13,9},{6,2},{10,6},{14,10},{7,3},{... | collective-permute-start | bytes 1179656 | tf_op jit(solution)/shard_map/ppermute | solution.py:216
  299.1 14.7 %collective-permute-start.41 = (f32[128,768]{1,0:T(8,128)S(1)}, f32[128,768]{1,0:T(8,128)S(1)}, u32[]{:S(2)}, u32[]{:S(2)}) collective-permute-start(f32[128,768]{1,0:T(8,128)S(1)} %collective-permute-done.40.refs_5_), channel_id=1, source_target_pairs={{0,4},{4,8},{8,12},{1,5},{5,9},{9,13},{2,6},{6,10},{10,14},{3,7},{... | collective-permute-start | bytes 1179656 | tf_op jit(solution)/shard_map/ppermute | solution.py:216
  305.7 11.1 %collective-permute-start.42 = (f32[128,768]{1,0:T(8,128)}, f32[128,768]{1,0:T(8,128)S(1)}, u32[]{:S(2)}, u32[]{:S(2)}) collective-permute-start(f32[128,768]{1,0:T(8,128)} %copy-done.51), channel_id=1, source_target_pairs={{4,0},{8,4},{12,8},{5,1},{9,5},{13,9},{6,2},{10,6},{14,10},{7,3},{... | collective-permute-start | bytes 1179656 | tf_op jit(solution)/shard_map/ppermute | solution.py:216
  307.0 11.2 %collective-permute-start.43 = (f32[128,768]{1,0:T(8,128)}, f32[128,768]{1,0:T(8,128)}, u32[]{:S(2)}, u32[]{:S(2)}) collective-permute-start(f32[128,768]{1,0:T(8,128)} %copy-done.50), channel_id=1, source_target_pairs={{0,4},{4,8},{8,12},{1,5},{5,9},{9,13},{2,6},{6,10},{10,14},{3,7},{... | collective-permute-start | bytes 1179656 | tf_op jit(solution)/shard_map/ppermute | solution.py:216
  321.6 2.3 collective-permute-start.44
  321.7 12.2 %collective-permute-start.45 = (f32[128,768]{1,0:T(8,128)}, f32[128,768]{1,0:T(8,128)S(1)}, u32[]{:S(2)}, u32[]{:S(2)}) collective-permute-start(f32[128,768]{1,0:T(8,128)} %get-tuple-element.43), channel_id=1, source_target_pairs={{0,2},{1,3},{2,0},{3,1},{4,6},{5,7},{6,4},{7,5},{8,10},{9,11},{10,... | collective-permute-start | bytes 1179656 | tf_op jit(solution)/shard_map/ppermute | solution.py:168
  323.3 18.2 %collective-permute-start.46 = (f32[128,768]{1,0:T(8,128)}, f32[128,768]{1,0:T(8,128)S(1)}, u32[]{:S(2)}, u32[]{:S(2)}) collective-permute-start(f32[128,768]{1,0:T(8,128)} %get-tuple-element.44), channel_id=1, source_target_pairs={{0,3},{1,2},{2,1},{3,0},{4,7},{5,6},{6,5},{7,4},{8,11},{9,10},{10,... | collective-permute-start | bytes 1179656 | tf_op jit(solution)/shard_map/ppermute | solution.py:168
  323.5 71.3 %collective-permute-start.29 = (f32[384,768]{1,0:T(8,128)S(1)}, f32[384,768]{1,0:T(8,128)}, u32[]{:S(2)}, u32[]{:S(2)}) collective-permute-start(f32[384,768]{1,0:T(8,128)S(1)} %pad_maximum_fusion.refs_1_), channel_id=1, source_target_pairs={{0,1},{1,0},{2,3},{3,2},{4,5},{5,4},{6,7},{7,6},{8,9},{9,8},{10,11... | collective-permute-start | bytes 3538952 | tf_op jit(solution)/shard_map/ppermute | solution.py:168
  323.9 39.0 %collective-permute-start.50 = (f32[128,768]{1,0:T(8,128)}, f32[128,768]{1,0:T(8,128)}, u32[]{:S(2)}, u32[]{:S(2)}) collective-permute-start(f32[128,768]{1,0:T(8,128)} %get-tuple-element.50), channel_id=1, source_target_pairs={{0,1},{1,0},{2,3},{3,2},{4,5},{5,4},{6,7},{7,6},{8,9},{9,8},{10,11... | collective-permute-start | bytes 1179656 | tf_op jit(solution)/shard_map/ppermute | solution.py:168
  333.9 29.6 %collective-permute-start.51 = (f32[128,768]{1,0:T(8,128)}, f32[128,768]{1,0:T(8,128)}, u32[]{:S(2)}, u32[]{:S(2)}) collective-permute-start(f32[128,768]{1,0:T(8,128)} %get-tuple-element.51), channel_id=1, source_target_pairs={{0,2},{1,3},{2,0},{3,1},{4,6},{5,7},{6,4},{7,5},{8,10},{9,11},{10,... | collective-permute-start | bytes 1179656 | tf_op jit(solution)/shard_map/ppermute | solution.py:168
  341.5 23.3 %collective-permute-start.52 = (f32[128,768]{1,0:T(8,128)}, f32[128,768]{1,0:T(8,128)}, u32[]{:S(2)}, u32[]{:S(2)}) collective-permute-start(f32[128,768]{1,0:T(8,128)} %get-tuple-element.52), channel_id=1, source_target_pairs={{0,3},{1,2},{2,1},{3,0},{4,7},{5,6},{6,5},{7,4},{8,11},{9,10},{10,... | collective-permute-start | bytes 1179656 | tf_op jit(solution)/shard_map/ppermute | solution.py:168
  362.8 18.6 %collective-permute-start.47 = (f32[128,768]{1,0:T(8,128)}, f32[128,768]{1,0:T(8,128)S(1)}, u32[]{:S(2)}, u32[]{:S(2)}) collective-permute-start(f32[128,768]{1,0:T(8,128)} %get-tuple-element.46), channel_id=1, source_target_pairs={{0,1},{1,0},{2,3},{3,2},{4,5},{5,4},{6,7},{7,6},{8,9},{9,8},{10,11... | collective-permute-start | bytes 1179656 | tf_op jit(solution)/shard_map/ppermute | solution.py:168
  362.9 18.5 %collective-permute-start.48 = (f32[128,768]{1,0:T(8,128)}, f32[128,768]{1,0:T(8,128)S(1)}, u32[]{:S(2)}, u32[]{:S(2)}) collective-permute-start(f32[128,768]{1,0:T(8,128)} %get-tuple-element.47), channel_id=1, source_target_pairs={{0,2},{1,3},{2,0},{3,1},{4,6},{5,7},{6,4},{7,5},{8,10},{9,11},{10,... | collective-permute-start | bytes 1179656 | tf_op jit(solution)/shard_map/ppermute | solution.py:168
  363.4 19.2 %collective-permute-start.49 = (f32[128,768]{1,0:T(8,128)}, f32[128,768]{1,0:T(8,128)S(1)}, u32[]{:S(2)}, u32[]{:S(2)}) collective-permute-start(f32[128,768]{1,0:T(8,128)} %get-tuple-element.48), channel_id=1, source_target_pairs={{0,3},{1,2},{2,1},{3,0},{4,7},{5,6},{6,5},{7,4},{8,11},{9,10},{10,... | collective-permute-start | bytes 1179656 | tf_op jit(solution)/shard_map/ppermute | solution.py:168
  394.5 13.4 %collective-permute-start.53 = (f32[384,768]{1,0:T(8,128)S(1)}, f32[384,768]{1,0:T(8,128)S(1)}, u32[]{:S(2)}, u32[]{:S(2)}) collective-permute-start(f32[384,768]{1,0:T(8,128)S(1)} %slice.113), channel_id=1, source_target_pairs={{0,1},{1,0},{2,3},{3,2},{4,5},{5,4},{6,7},{7,6},{8,9},{9,8},{10,11... | collective-permute-start | bytes 3538952 | tf_op jit(solution)/shard_map/ppermute | solution.py:168
  408.0 28.4 %collective-permute-start.55 = (f32[384,768]{1,0:T(8,128)S(1)}, f32[384,768]{1,0:T(8,128)S(1)}, u32[]{:S(2)}, u32[]{:S(2)}) collective-permute-start(f32[384,768]{1,0:T(8,128)S(1)} %slice_add_fusion.refs_12_), channel_id=1, source_target_pairs={{0,2},{1,3},{2,0},{3,1},{4,6},{5,7},{6,4},{7,5},{8,10},{9,11},{10,... | collective-permute-start | bytes 3538952 | tf_op jit(solution)/shard_map/ppermute | solution.py:168
  433.5 1.8 collective-permute-start.54
  433.8 2.0 collective-permute-start.57
  434.0 2.3 collective-permute-start.56
  (61 other events, 406.0 us)
Sparse Core Ops, SparseCore 0:
  40.1 46.9 all-gather.4
  254.9 47.1 all-gather.6
